TPU v7x, 256 devices: a whole 4x4x8 slice. The times are simulated.
256 devices in a mesh: grp: 4 (over x), grid: 64 (over y, z, core).
Axes of the slice: x: 4, y: 4, z: 8, core: 2. Of those that a mesh axis runs over, the one named last changes fastest.
Arguments:
- orbitals: float32 [512, 262144], P('grp', 'grid'), may hold values from -6 to 6
- anchors: int32 [512, 3], replicated, may hold values from 0 to 31
- pair_slots: int32 [256, 4, 2], replicated, may hold values from -1 to 511, as said below
Outputs:
- exchange_term: float32 [512, 262144], P('grp', 'grid')
Inputs may be any that keep to these rules, and one draw needn't show every extreme that they name: `pair_slots`: row k lists the pairs of owner k, the device with index k in the order grp, grid; its first slots hold pairs of two different orbital numbers and its other slots hold -1 in both columns. Exactly 512 slots hold pairs in all, no row holds more than 4, and some row holds exactly 4.
All inputs are finite; a program needn't handle non-finite values.
Results may differ from a plain program's by a relative error of at most 0.0003.
Values sent between devices are 32-bit elements; how exact they have to be, the bound alone decides.
No kernel may reach another device: no remote copies, remote signals or barrier semaphores. Data moves between devices by JAX's collectives and lax.ppermute only.
A program may use at most 128 MiB of HBM per device.

v0:
```python
import functools

import jax
import jax.numpy as jnp
from jax import lax
from jax.experimental import pallas as pl
from jax.experimental.pallas import tpu as pltpu
from jax.sharding import PartitionSpec as P

B = 64
PAIR_DEV = 2
ITERS = 3
ROWS = B * B // 128
KEEP = 48
UNROLL = 8


def shift_field(field, offset, extent):
    plane_size = extent * extent
    padded_x = jnp.pad(field, ((extent, extent), (0, 0)))
    moved = lax.dynamic_slice_in_dim(padded_x, extent - offset[0], extent, 0)
    padded_yz = jnp.pad(moved, ((0, 0), (plane_size, plane_size)))
    linear = offset[1] * extent + offset[2]
    moved = lax.dynamic_slice_in_dim(padded_yz, plane_size - linear, plane_size, 1)
    cells = lax.broadcasted_iota(jnp.int32, (1, plane_size), 1)
    coord_y = cells // extent - offset[1]
    coord_z = cells % extent - offset[2]
    inside = (coord_y >= 0) & (coord_y < extent) & (coord_z >= 0) & (coord_z < extent)
    return jnp.where(inside, moved, jnp.zeros_like(moved))


def operate(field, extent):
    padded_x = jnp.pad(field, ((1, 1), (0, 0)))
    beside = padded_x[2:] + padded_x[:-2]
    padded_y = jnp.pad(field, ((0, 0), (extent, extent)))
    beside = beside + padded_y[:, 2 * extent :] + padded_y[:, : -2 * extent]
    padded_z = jnp.pad(field, ((0, 0), (1, 1)))
    cells = lax.broadcasted_iota(jnp.int32, (1, field.shape[1]), 1) % extent
    upper_z = jnp.where(cells < extent - 1, padded_z[:, 2:], jnp.zeros_like(field))
    lower_z = jnp.where(cells > 0, padded_z[:, :-2], jnp.zeros_like(field))
    return 6.0 * field - beside - upper_z - lower_z


def conjugate(density, extent):
    potential = jnp.zeros_like(density)
    resid = density
    direction = density
    norm_now = jnp.sum(resid * resid)
    for turn in range(ITERS):
        image = operate(direction, extent)
        step_len = norm_now / jnp.sum(direction * image)
        potential = potential + step_len * direction
        resid = resid - step_len * image
        norm_next = jnp.sum(resid * resid)
        direction = resid + norm_next / norm_now * direction
        norm_now = norm_next
    return potential


def pair_terms(field_a, field_b, offset, extent):
    partner = shift_field(field_b, offset, extent)
    density = field_a * partner
    potential = conjugate(density, extent)
    term_a = potential * partner
    term_b = shift_field(potential * field_a, -offset, extent)
    return (term_a, term_b)


def deal_evenly(pair_slots, owner_count, each_owner):
    flat_slots = pair_slots.reshape(-1, 2)
    filled = (flat_slots[:, 0] >= 0).astype(jnp.int32)
    order = jnp.arange(flat_slots.shape[0], dtype=jnp.int32)
    position = jnp.sum(jnp.where(order[None, :] < order[:, None], filled[None, :], 0), axis=1)
    wanted = lax.broadcasted_iota(jnp.int32, (owner_count, each_owner), 1) * owner_count
    wanted = (wanted + lax.broadcasted_iota(jnp.int32, (owner_count, each_owner), 0)).reshape(-1)
    matched = (position[None, :] == wanted[:, None]) & (filled[None, :] == 1)
    picked = jnp.dot(matched.astype(jnp.int32), flat_slots)
    return picked.reshape(owner_count, each_owner, 2)


def general(orbitals, anchors, pair_slots):
    extent = B
    grid_count = lax.axis_size("grid")
    owner_count = lax.axis_size("grp") * grid_count
    group_idx = lax.axis_index("grp")
    place_idx = lax.axis_index("grid")
    assignment = deal_evenly(pair_slots, owner_count, PAIR_DEV)
    filled = assignment[..., 0] >= 0
    safe_ids = jnp.maximum(assignment, 0)
    pieces = lax.all_gather(orbitals, "grp", axis=0, tiled=True)
    group_table = lax.dynamic_slice_in_dim(safe_ids, group_idx * grid_count, grid_count, 0)
    gather_ids = jnp.transpose(group_table, (1, 2, 0))
    outgoing = pieces[gather_ids]
    arrived = lax.all_to_all(outgoing, "grid", split_axis=2, concat_axis=2, tiled=True)
    owner_idx = group_idx * grid_count + place_idx
    own_pairs = safe_ids[owner_idx]
    own_filled = filled[owner_idx]
    offsets = anchors[own_pairs[:, 1]] - anchors[own_pairs[:, 0]]

    def solve_slot(slot_item):
        boxes_pair, offset, flag = slot_item
        term_a, term_b = pair_terms(boxes_pair[0], boxes_pair[1], offset, extent)
        weight_flag = jnp.where(flag, 1.0, 0.0).astype(jnp.float32)
        return jnp.stack([term_a, term_b]) * weight_flag

    terms = lax.map(solve_slot, (arrived, offsets, own_filled))
    returned = lax.all_to_all(terms, "grid", split_axis=2, concat_axis=2, tiled=True)
    flat_terms = returned.reshape(-1, returned.shape[-1])
    summed = jax.ops.segment_sum(flat_terms, gather_ids.reshape(-1), num_segments=anchors.shape[0])
    return lax.psum_scatter(summed, "grp", scatter_dimension=0, tiled=True)


def route_kernel(me_ref, a_ref, b_ref, pos_ref, slot_ref, fits_ref):
    me = me_ref[0]
    a, b = a_ref[...], b_ref[...]
    n = a.shape[0]
    f32, i32 = jnp.float32, jnp.int32
    groups, each = 4, 2 * B

    def col(x):
        return jnp.sum(x, axis=1, keepdims=True)

    before = lax.broadcasted_iota(i32, (n, n), 0) > lax.broadcasted_iota(i32, (n, n), 1)
    before = jnp.where(before, 1.0, 0.0).astype(jnp.bfloat16)

    def rank_in(hot):
        return col(jnp.dot(before, hot.astype(jnp.bfloat16), preferred_element_type=f32) * hot).astype(i32)

    lane = lax.broadcasted_iota(i32, (n, 128), 1)
    valid = a >= 0
    ga, gb = a >> 7, b >> 7
    low, high = jnp.minimum(ga, gb), jnp.maximum(ga, gb)
    hot = jnp.where(valid & (lane == low * groups + high), 1.0, 0.0)
    rank = rank_in(hot)

    sums = jnp.sum(hot, axis=0, keepdims=True).astype(i32)
    lane1 = lax.broadcasted_iota(i32, (1, 128), 1)
    count, up = {}, {}
    for g in range(groups):
        for h in range(g, groups):
            count[g, h] = jnp.sum(jnp.where(lane1 == g * groups + h, sums, 0))
            up[g, h] = (count[g, h] >> 1) if h > g else 0

    def loads():
        load = [0] * groups
        for (g, h), c in count.items():
            load[g] = load[g] + (c - up[g, h])
            load[h] = load[h] + up[g, h]
        return load

    load = loads()
    for g, h in count:
        if h > g:
            up[g, h] = up[g, h] + ((load[g] - load[h] + 2) >> 2)
    load = loads()
    excess = 0
    for g in range(groups - 1):
        excess = excess + load[g] - each
        up[g, g + 1] = up[g, g + 1] + excess
    fits = 1
    goes_up = jnp.zeros((1, 128), i32)
    for (g, h), c in count.items():
        if h > g:
            u = up[g, h]
            fine = (u >= 0) & (u <= KEEP) & (c - u >= 0) & (c - u <= KEEP)
            fits = jnp.where(fine, fits, 0)
            goes_up = jnp.where(lane1 == g * groups + h, u, goes_up)
    fits_ref[0] = fits

    ups = col(hot * goes_up.astype(f32)).astype(i32)
    rises = rank < ups
    group = jnp.where(rises, high, low)
    source = low + high - group
    crosses = valid & (low != high)
    hot = jnp.where(valid & (lane == group), 1.0, 0.0)
    q = rank_in(hot)
    put = (((group - source) & 3) - 1) * KEEP + jnp.where(rises, rank, rank - ups)
    near_b = ga != group
    near = jnp.where(near_b, b, a) & 127
    far = jnp.where(near_b, a, b) & 127
    table = jnp.where(crosses, 128 + put, far)

    def side(*columns):
        at = lax.broadcasted_iota(i32, (n, 8), 1)
        out = jnp.zeros((n, 8), f32)
        for k, column in enumerate(columns):
            out = jnp.where(at == k, column.astype(f32), out)
        return out.astype(jnp.bfloat16)

    def spread(columns, mask):
        hot = jnp.where(mask, 1.0, 0.0).astype(jnp.bfloat16)
        out = lax.dot_general(columns, hot, (((0,), (0,)), ((), ())), preferred_element_type=f32)
        return out.astype(i32)

    mine = valid & (group == me)
    flag = jnp.where(near_b, 1, 0)
    columns = side(near, table & 255, a & 255, b & 255, flag, table >> 8, a >> 8, b >> 8)
    got = spread(columns, mine & (lane == q))
    pos_ref[...] = got
    pos_ref[1:4] = got[1:4] + 256 * got[5:8]
    wide = lax.broadcasted_iota(i32, (n, slot_ref.shape[1]), 1)
    here = wide == put
    zero = jnp.zeros_like(a)
    slots = spread(side(far, zero, zero + 1), crosses & (source == me) & here)
    slot_ref[...] = slots + spread(side(zero, q), crosses & mine & here)


def route(me, pair_slots):
    flat = pair_slots.reshape(-1, 2)
    width = 128 * -(-(3 * KEEP) // 128)
    vmem, smem = pl.BlockSpec(memory_space=pltpu.VMEM), pl.BlockSpec(memory_space=pltpu.SMEM)
    return pl.pallas_call(
        route_kernel,
        out_shape=[
            jax.ShapeDtypeStruct((8, 128), jnp.int32),
            jax.ShapeDtypeStruct((8, width), jnp.int32),
            jax.ShapeDtypeStruct((1,), jnp.int32),
        ],
        in_specs=[smem, vmem, vmem],
        out_specs=[vmem, vmem, smem],
        compiler_params=pltpu.CompilerParams(vmem_limit_bytes=40 << 20),
        cost_estimate=pl.CostEstimate(flops=10_000_000, bytes_accessed=1_000_000, transcendentals=0),
        name="route",
    )(me, flat[:, :1], flat[:, 1:])


def fetch_kernel(row_of, first, tables, idx_ref, *refs):
    parts, (*outs, table, sem) = refs[:tables], refs[tables:]
    copies, end = [], 0
    for k, part in enumerate(parts):
        copies.append(pltpu.make_async_copy(part, table.at[pl.ds(end, part.shape[0])], sem.at[k]))
        end += part.shape[0]
    for copy in copies:
        copy.start()
    for copy in copies:
        copy.wait()
    for k, out_ref in enumerate(outs):
        count = out_ref.shape[0]

        def move(i, carry, out_ref=out_ref, k=k, count=count):
            out_ref[i] = table[row_of(idx_ref, first + k * count, i)]
            return carry

        lax.fori_loop(0, count, move, 0, unroll=4)


def fetch(idx, tables, outs, count, row_of, first, name):
    rows = sum(t.shape[0] for t in tables)
    return pl.pallas_call(
        functools.partial(fetch_kernel, row_of, first, len(tables)),
        out_shape=[jax.ShapeDtypeStruct((count, ROWS, 128), jnp.float32)] * outs,
        in_specs=[pl.BlockSpec(memory_space=pltpu.SMEM)] + [pl.BlockSpec(memory_space=pl.ANY)] * len(tables),
        out_specs=[pl.BlockSpec(memory_space=pltpu.VMEM)] * outs,
        scratch_shapes=[pltpu.VMEM((rows, ROWS, 128), jnp.float32), pltpu.SemaphoreType.DMA((len(tables),))],
        compiler_params=pltpu.CompilerParams(vmem_limit_bytes=16 << 20),
        cost_estimate=pl.CostEstimate(flops=0, bytes_accessed=(rows + count * outs) * 16384, transcendentals=0),
        name=name,
    )(idx, *tables)


def solve_pair(orb_a, orb_b, anchor_ref, box_a, box_b, term_a, term_b, part, dens, resid, second, third, image):
    ox, oy, oz = [anchor_ref[3 * orb_b + k] - anchor_ref[3 * orb_a + k] for k in range(3)]
    shape = (ROWS, 128)
    line = lax.broadcasted_iota(jnp.int32, shape, 0)
    lane = lax.broadcasted_iota(jnp.int32, shape, 1)
    cy = 2 * line + (lane >> 6)
    cz = lane & 63
    low = lane < 64
    no_y = ((cy == 0) | (cy == B - 1))
    no_up, no_down = cz == B - 1, cz == 0

    def shifter(sy, sz):
        flat = (sy * B + sz + B * B) & (B * B - 1)
        lines, steps = flat >> 7, flat & 127
        inside = (cy >= sy) & (cy < B + sy) & (cz >= sz) & (cz < B + sz)
        keep = lane >= steps

        def shift(plane):
            turned = pltpu.roll(plane, steps, axis=1)
            turned = jnp.where(keep, turned, pltpu.roll(turned, 1, axis=0))
            return jnp.where(inside, pltpu.roll(turned, lines, axis=0), 0.0)

        return shift

    def apply(ref, x):
        here = ref[x + 1]
        swapped = pltpu.roll(here, 64, axis=1)
        other = jnp.where(low, pltpu.roll(swapped, 1, axis=0), pltpu.roll(swapped, ROWS - 1, axis=0))
        beside = ref[x] + ref[x + 2] + swapped + jnp.where(no_y, 0.0, other)
        upper = jnp.where(no_up, 0.0, pltpu.roll(here, 127, axis=1))
        lower = jnp.where(no_down, 0.0, pltpu.roll(here, 1, axis=1))
        return here, 6.0 * here - beside - upper - lower

    zero = jnp.zeros(shape, jnp.float32)
    for ref in (dens, second, third):
        ref[0] = zero
        ref[B + 1] = zero

    def total(x):
        return jnp.sum(x, keepdims=True)

    def planes(step, init=None):
        return lax.fori_loop(0, B, step, zero if init is None else init, unroll=UNROLL)

    shift_on = shifter(oy, oz)
    shift_back = shifter(-oy, -oz)

    def begin(x, acc):
        src = x - ox
        inside = jnp.where((src >= 0) & (src < B), 1.0, 0.0)
        moved = shift_on(box_b[jnp.clip(src, 0, B - 1)]) * inside
        density = box_a[x] * moved
        part[x] = moved
        dens[x + 1] = density
        return acc + density * density

    norm0 = total(planes(begin))

    def first(x, acc):
        here, img = apply(dens, x)
        image[x] = img
        return acc + here * img

    step0 = norm0 / total(planes(first))

    def rest0(x, acc):
        left = dens[x + 1] - step0 * image[x]
        resid[x] = left
        return acc + left * left

    norm1 = total(planes(rest0))
    ratio0 = norm1 / norm0

    def turn1(x, acc):
        second[x + 1] = resid[x] + ratio0 * dens[x + 1]
        return acc

    planes(turn1)

    def again(x, acc):
        here, img = apply(second, x)
        image[x] = img
        return acc + here * img

    step1 = norm1 / total(planes(again))

    def rest1(x, acc):
        left = resid[x] - step1 * image[x]
        resid[x] = left
        return acc + left * left

    norm2 = total(planes(rest1))
    ratio1 = norm2 / norm1

    def turn2(x, acc):
        third[x + 1] = resid[x] + ratio1 * second[x + 1]
        return acc

    planes(turn2)

    def last(x, acc):
        here, img = apply(third, x)
        return acc + here * img

    step2 = norm2 / total(planes(last))

    def finish(x, acc):
        potential = step0 * dens[x + 1] + step1 * second[x + 1] + step2 * third[x + 1]
        term_a[x] = potential * part[x]
        image[x] = potential * box_a[x]
        return acc

    planes(finish)

    def back(x, acc):
        src = x + ox
        inside = jnp.where((src >= 0) & (src < B), 1.0, 0.0)
        term_b[x] = shift_back(image[jnp.clip(src, 0, B - 1)]) * inside
        return acc

    planes(back)


def pair_kernel(place_ref, pos_ref, anchor_ref, near_ref, far_ref, near_out, far_out, boxes, terms, *rest):
    *fields, sem_in, sem_out = rest
    at = [s * B + place_ref[0] for s in range(PAIR_DEV)]
    flags = [pos_ref[4, k] for k in at]

    def pulls(s):
        return [
            pltpu.make_async_copy(near_ref.at[:, s], boxes.at[s, flags[s]], sem_in.at[s, 0]),
            pltpu.make_async_copy(far_ref.at[:, s], boxes.at[s, 1 - flags[s]], sem_in.at[s, 1]),
        ]

    def pushes(s):
        return [
            pltpu.make_async_copy(terms.at[s, flags[s]], near_out.at[:, s], sem_out.at[s, 0]),
            pltpu.make_async_copy(terms.at[s, 1 - flags[s]], far_out.at[:, s], sem_out.at[s, 1]),
        ]

    for s in range(PAIR_DEV):
        for copy in pulls(s):
            copy.start()
    for s in range(PAIR_DEV):
        for copy in pulls(s):
            copy.wait()
        solve_pair(
            pos_ref[2, at[s]], pos_ref[3, at[s]], anchor_ref,
            boxes.at[s, 0], boxes.at[s, 1], terms.at[s, 0], terms.at[s, 1], *fields,
        )
        for copy in pushes(s):
            copy.start()
    for s in range(PAIR_DEV):
        for copy in pushes(s):
            copy.wait()


def solve(place, pos, anchors, near, far):
    smem = pl.BlockSpec(memory_space=pltpu.SMEM)
    anywhere = pl.BlockSpec(memory_space=pl.ANY)
    field = pltpu.VMEM((B, ROWS, 128), jnp.float32)
    padded = pltpu.VMEM((B + 2, ROWS, 128), jnp.float32)
    two = pltpu.VMEM((PAIR_DEV, 2, B, ROWS, 128), jnp.float32)
    dma = pltpu.SemaphoreType.DMA((PAIR_DEV, 2))
    return pl.pallas_call(
        pair_kernel,
        out_shape=[jax.ShapeDtypeStruct((B, PAIR_DEV, ROWS, 128), jnp.float32)] * 2,
        in_specs=[smem, smem, smem, anywhere, anywhere],
        out_specs=[anywhere, anywhere],
        scratch_shapes=[two, two, field, padded, field, padded, padded, field, dma, dma],
        compiler_params=pltpu.CompilerParams(vmem_limit_bytes=32 << 20),
        cost_estimate=pl.CostEstimate(flops=100_000_000, bytes_accessed=30_000_000, transcendentals=0),
        name="solve",
    )(place, pos, anchors, near, far)


def add_far_kernel(pos_ref, slot_ref, terms_ref, *refs):
    *from_groups, out_ref = refs
    out_ref[...] = jnp.zeros(out_ref.shape, jnp.float32)

    def here(p, carry):
        for s in range(PAIR_DEV):
            j = pos_ref[1, s * B + p]

            @pl.when(j < 128)
            def _(j=j, s=s):
                out_ref[j] = out_ref[j] + terms_ref[p, s]

        return carry

    lax.fori_loop(0, B, here, 0)

    def there(k, carry):
        for d, ref in enumerate(from_groups):
            at = d * KEEP + k

            @pl.when(slot_ref[2, at] == 1)
            def _(at=at, ref=ref):
                j = slot_ref[0, at]
                out_ref[j] = out_ref[j] + ref[k]

        return carry

    lax.fori_loop(0, KEEP, there, 0)


def add_far(pos, slot, terms, from_groups):
    smem, vmem = pl.BlockSpec(memory_space=pltpu.SMEM), pl.BlockSpec(memory_space=pltpu.VMEM)
    return pl.pallas_call(
        add_far_kernel,
        out_shape=jax.ShapeDtypeStruct((128, ROWS, 128), jnp.float32),
        in_specs=[smem, smem] + [vmem] * 4,
        out_specs=vmem,
        compiler_params=pltpu.CompilerParams(vmem_limit_bytes=24 << 20),
        cost_estimate=pl.CostEstimate(flops=2_000_000, bytes_accessed=10_000_000, transcendentals=0),
        name="add_far",
    )(pos, slot, terms, *from_groups)


def add_near_kernel(pos_ref, sum_ref, terms_ref, out_ref, acc):
    acc[...] = sum_ref[...]

    def here(p, carry):
        for s in range(PAIR_DEV):
            j = pos_ref[0, s * B + p]
            acc[j] = acc[j] + terms_ref[p, s]
        return carry

    lax.fori_loop(0, B, here, 0)
    for j in range(ROWS):
        out_ref[:, j * 128 : (j + 1) * 128] = acc[:, j, :]


def add_near(pos, summed, terms):
    smem, vmem = pl.BlockSpec(memory_space=pltpu.SMEM), pl.BlockSpec(memory_space=pltpu.VMEM)
    return pl.pallas_call(
        add_near_kernel,
        out_shape=jax.ShapeDtypeStruct((128, ROWS * 128), jnp.float32),
        in_specs=[smem, vmem, vmem],
        out_specs=vmem,
        scratch_shapes=[pltpu.VMEM((128, ROWS, 128), jnp.float32)],
        compiler_params=pltpu.CompilerParams(vmem_limit_bytes=24 << 20),
        cost_estimate=pl.CostEstimate(flops=2_000_000, bytes_accessed=10_000_000, transcendentals=0),
        name="add_near",
    )(pos, summed, terms)


def turned(x, shift):
    groups = lax.axis_size("grp")
    return lax.ppermute(x, "grp", [(g, (g + shift) % groups) for g in range(groups)])


def near_row(pos, first, i):
    return pos[0, (i & 1) * B + (i >> 1)]


def far_row(pos, first, i):
    return pos[1, (i & 1) * B + (i >> 1)]


def sent_row(slot, first, i):
    return slot[0, first + i]


def used_row(slot, first, i):
    q = slot[1, first + i]
    return 2 * (q & (B - 1)) + (q >> 6)


def exchanged(planes):
    return lax.all_to_all(planes.reshape(B, PAIR_DEV, ROWS, 128), "grid", 0, 0, tiled=True)


def fitting(orbitals, anchors, place, pos, slot):
    local = orbitals.reshape(128, ROWS, 128)
    near = exchanged(*fetch(pos, [local], 1, 2 * B, near_row, 0, "deal_near"))
    sent = fetch(slot, [local], 3, KEEP, sent_row, 0, "send")
    arrived = [turned(x, d) for d, x in enumerate(sent, 1)]
    far = exchanged(*fetch(pos, [local] + arrived, 1, 2 * B, far_row, 0, "deal_far"))
    near_terms, far_terms = solve(place, pos, anchors.reshape(-1), near, far)
    far_terms = exchanged(far_terms)
    back = fetch(slot, [far_terms.reshape(2 * B, ROWS, 128)], 3, KEEP, used_row, 0, "back")
    from_groups = [turned(x, -d) for d, x in enumerate(back, 1)]
    near_terms = exchanged(near_terms)
    return add_near(pos, add_far(pos, slot, far_terms, from_groups), near_terms)


def body(orbitals, anchors, pair_slots):
    me = lax.axis_index("grp").astype(jnp.int32)[None]
    place = lax.axis_index("grid").astype(jnp.int32)[None]
    pos, slot, fits = route(me, pair_slots)
    return lax.cond(
        fits[0] == 1,
        lambda: fitting(orbitals, anchors, place, pos, slot),
        lambda: general(orbitals, anchors, pair_slots),
    )


def solution(mesh):
    return jax.shard_map(
        body,
        mesh=mesh,
        in_specs=(P("grp", "grid"), P(), P()),
        out_specs=P("grp", "grid"),
        check_vma=False,
    )
```

profile of v0, /device:TPU:1, one launch (start us, length us, event | category | flops | bytes accessed | tf_op | source)
XLA Modules:
  0.0 285.6 jit_solution(2848713848741598709)
XLA Ops:
  7.8 4.6 %route.1 = (s32[8,128]{1,0:T(8,128)S(1)}, s32[8,256]{1,0:T(8,128)S(1)}, s32[1]{0:T(128)}) custom-call(s32[1]{0:T(128)} %bitcast.21.me_ref, s32[1024,1]{1,0:T(8,128)S(1)} %get-tuple-element.241.a_ref, s32[1024,1]{1,0:T(8,128)S(1)} %get-tuple-element.240.b_ref), custom_call_target="tpu_custom_call" | custom-call | flops 10000000 | bytes 1000000 | tf_op jit(solution)/shard_map/route/pallas_call | solution.py:212
  13.0 265.8 %conditional.1 = (f32[128,4096]{1,0:T(8,128)}) conditional(s32[]{:T(128)} %bitcast.23, (s32[256,4,2]{0,2,1:T(2,128)S(1)}, f32[128,4096]{1,0:T(8,128)}, s32[512,3]{0,1:T(4,128)S(1)}) %tuple.93, (s32[512,3]{0,1:T(4,128)S(1)}, f32[128,4096]{1,0:T(8,128)}, s32[8,128]{1,0:T(8,128)S(1)}, s32[8,256]{1,0:T(8,128)S(1)}, s32[]{:T(128)}) %tuple.94), branch_computations={%region_0.12_spmd, %region_12.13_spmd} | conditional | flops 104000000 | bytes 185787872 | solution.py:552
  13.2 2.0 copy.41
  17.7 13.3 %all-to-all-start = ((f32[64,2,32,128]{3,2,1,0:T(8,128)}), f32[64,2,32,128]{3,2,1,0:T(8,128)}, u32[]{:S(2)}, u32[]{:S(2)}) async-start(f32[64,2,32,128]{3,2,1,0:T(8,128)} %bitcast.72), calls=%async_computation | async-start | bytes 4194304 | tf_op jit(solution)/shard_map/cond/branch_1_fun/all_to_all | solution.py:531
  31.0 1.3 send.1
  33.7 2.4 collective-permute-start.1
  37.3 15.1 %collective-permute-done.refs_1_ = f32[48,32,128]{2,1,0:T(8,128)S(1)} collective-permute-done((f32[48,32,128]{2,1,0:T(8,128)S(1)}, f32[48,32,128]{2,1,0:T(8,128)S(1)}, u32[]{:S(2)}, u32[]{:S(2)}) %collective-permute-start) | collective-permute-done | bytes 786464 | tf_op jit(solution)/shard_map/cond/branch_1_fun/ppermute | solution.py:510
  52.4 17.8 %collective-permute-done.1.refs_2_ = f32[48,32,128]{2,1,0:T(8,128)S(1)} collective-permute-done((f32[48,32,128]{2,1,0:T(8,128)S(1)}, f32[48,32,128]{2,1,0:T(8,128)S(1)}, u32[]{:S(2)}, u32[]{:S(2)}) %collective-permute-start.1) | collective-permute-done | bytes 786464 | tf_op jit(solution)/shard_map/cond/branch_1_fun/ppermute | solution.py:510
  70.2 1.6 deal_far.1
  73.1 9.1 %all-to-all-done.near_ref = f32[64,2,32,128]{3,2,1,0:T(8,128)} async-done(((f32[64,2,32,128]{3,2,1,0:T(8,128)}), f32[64,2,32,128]{3,2,1,0:T(8,128)}, u32[]{:S(2)}, u32[]{:S(2)}) %all-to-all-start) | async-done | bytes 2097184 | tf_op jit(solution)/shard_map/cond/branch_1_fun/all_to_all | solution.py:531
  82.2 5.8 %all-to-all-start.1 = ((f32[64,2,32,128]{3,2,1,0:T(8,128)}), f32[64,2,32,128]{3,2,1,0:T(8,128)S(1)}, u32[]{:S(2)}, u32[]{:S(2)}) async-start(f32[64,2,32,128]{3,2,1,0:T(8,128)} %bitcast.73), calls=%async_computation.1 | async-start | bytes 4194304 | tf_op jit(solution)/shard_map/cond/branch_1_fun/all_to_all | solution.py:531
  88.4 50.9 %all-to-all-done.1.far_ref = f32[64,2,32,128]{3,2,1,0:T(8,128)S(1)} async-done(((f32[64,2,32,128]{3,2,1,0:T(8,128)}), f32[64,2,32,128]{3,2,1,0:T(8,128)S(1)}, u32[]{:S(2)}, u32[]{:S(2)}) %all-to-all-start.1) | async-done | bytes 2097184 | tf_op jit(solution)/shard_map/cond/branch_1_fun/all_to_all | solution.py:531
  139.3 18.4 %solve.1 = (f32[64,2,32,128]{3,2,1,0:T(8,128)S(1)}, f32[64,2,32,128]{3,2,1,0:T(8,128)S(1)}) custom-call(s32[1]{0:T(128)} %bitcast.17.place_ref, s32[8,128]{1,0:T(8,128)S(1)} %get-tuple-element.129.idx_ref.pos_ref, s32[1536]{0:T(1024)S(1)} %reshape.244.anchor_ref, f32[64,2,32,128]{3,2,1,0:T(8,128)} %all-to-all-done.near_ref, ...), custom_call_target="tpu_custom_call" | custom-call | flops 100000000 | bytes 30000000 | tf_op jit(solution)/shard_map/cond/branch_1_fun/solve/pallas_call | solution.py:425
  157.7 56.9 %all_to_all.24.terms_ref = f32[64,2,32,128]{3,2,1,0:T(8,128)S(1)} all-to-all(f32[64,2,32,128]{3,2,1,0:T(8,128)S(1)} %get-tuple-element.137), channel_id=1, replica_groups=mesh['grp'=4,'grid'=64] {'grid'}, dimensions={0} | all-to-all | bytes 4194304 | tf_op jit(solution)/shard_map/cond/branch_1_fun/all_to_all | solution.py:531
  214.5 6.0 %all-to-all-start.3 = ((f32[64,2,32,128]{3,2,1,0:T(8,128)}), f32[64,2,32,128]{3,2,1,0:T(8,128)}, u32[]{:S(2)}, u32[]{:S(2)}) async-start(f32[64,2,32,128]{3,2,1,0:T(8,128)} %copy-done.4), calls=%async_computation.3 | async-start | bytes 4194304 | tf_op jit(solution)/shard_map/cond/branch_1_fun/all_to_all | solution.py:531
  220.6 1.5 back.1
  222.1 2.6 collective-permute-start.3
  225.8 16.0 %collective-permute-done.3.refs_0_ = f32[48,32,128]{2,1,0:T(8,128)S(1)} collective-permute-done((f32[48,32,128]{2,1,0:T(8,128)S(1)}, f32[48,32,128]{2,1,0:T(8,128)S(1)}, u32[]{:S(2)}, u32[]{:S(2)}) %collective-permute-start.3) | collective-permute-done | bytes 786464 | tf_op jit(solution)/shard_map/cond/branch_1_fun/ppermute | solution.py:510
  241.8 2.7 collective-permute-done.4.refs_1_
  244.6 18.0 %collective-permute-done.5.refs_2_ = f32[48,32,128]{2,1,0:T(8,128)S(1)} collective-permute-done((f32[48,32,128]{2,1,0:T(8,128)S(1)}, f32[48,32,128]{2,1,0:T(8,128)S(1)}, u32[]{:S(2)}, u32[]{:S(2)}) %collective-permute-start.5) | collective-permute-done | bytes 786464 | tf_op jit(solution)/shard_map/cond/branch_1_fun/ppermute | solution.py:510
  262.6 4.8 %add_far.1.sum_ref = f32[128,32,128]{2,1,0:T(8,128)S(1)} custom-call(s32[8,128]{1,0:T(8,128)S(1)} %get-tuple-element.129.idx_ref.pos_ref, s32[8,256]{1,0:T(8,128)S(1)} %get-tuple-element.130.idx_ref.slot_ref, f32[64,2,32,128]{3,2,1,0:T(8,128)S(1)} %all_to_all.24.terms_ref, f32[48,32,128]{2,1,0:T(8,128)S(1)} %collective-permute-done.3.refs_0_, ...), custom_call_target="tpu_custom_call" | custom-call | flops 2000000 | bytes 10000000 | tf_op jit(solution)/shard_map/cond/branch_1_fun/add_far/pallas_call | solution.py:469
  268.7 3.1 %all-to-all-done.3.terms_ref = f32[64,2,32,128]{3,2,1,0:T(8,128)} async-done(((f32[64,2,32,128]{3,2,1,0:T(8,128)}), f32[64,2,32,128]{3,2,1,0:T(8,128)}, u32[]{:S(2)}, u32[]{:S(2)}) %all-to-all-start.3) | async-done | bytes 2097184 | tf_op jit(solution)/shard_map/cond/branch_1_fun/all_to_all | solution.py:531
  271.7 1.6 copy-done.3
  273.3 5.5 %add_near.1 = f32[128,4096]{1,0:T(8,128)} custom-call(s32[8,128]{1,0:T(8,128)S(1)} %get-tuple-element.129.idx_ref.pos_ref, f32[128,32,128]{2,1,0:T(8,128)S(1)} %copy-done.3, f32[64,2,32,128]{3,2,1,0:T(8,128)} %all-to-all-done.3.terms_ref), custom_call_target="tpu_custom_call" | custom-call | flops 2000000 | bytes 10000000 | tf_op jit(solution)/shard_map/cond/branch_1_fun/add_near/pallas_call | solution.py:496
  (23 shorter events, 10.3 us)
Async XLA Ops:
  6.5 6.4 %copy-start.8 = (s32[256,4,2]{0,2,1:T(2,128)S(1)}, s32[256,4,2]{0,2,1:T(2,128)}, u32[]{:S(2)}) copy-start(s32[256,4,2]{0,2,1:T(2,128)} %param.9) | copy-start | bytes 24580
  6.5 6.4 %copy-start.9 = (s32[512,3]{0,1:T(4,128)S(1)}, s32[512,3]{0,1:T(4,128)}, u32[]{:S(2)}) copy-start(s32[512,3]{0,1:T(4,128)} %param.8) | copy-start | bytes 18436
  16.4 1.3 copy-start
  17.7 64.5 %all-to-all-start = ((f32[64,2,32,128]{3,2,1,0:T(8,128)}), f32[64,2,32,128]{3,2,1,0:T(8,128)}, u32[]{:S(2)}, u32[]{:S(2)}) async-start(f32[64,2,32,128]{3,2,1,0:T(8,128)} %bitcast.72), calls=%async_computation | async-start | bytes 4194304 | tf_op jit(solution)/shard_map/cond/branch_1_fun/all_to_all | solution.py:531
  32.4 20.0 %collective-permute-start = (f32[48,32,128]{2,1,0:T(8,128)S(1)}, f32[48,32,128]{2,1,0:T(8,128)S(1)}, u32[]{:S(2)}, u32[]{:S(2)}) collective-permute-start(f32[48,32,128]{2,1,0:T(8,128)S(1)} %get-tuple-element.134), channel_id=1, source_target_pairs={{0,64},{64,128},{128,192},{192,0},{1,65},{65,129},{129,193},{193,1... | collective-permute-start | bytes 2359304 | tf_op jit(solution)/shard_map/cond/branch_1_fun/ppermute | solution.py:510
  33.7 36.5 %collective-permute-start.1 = (f32[48,32,128]{2,1,0:T(8,128)S(1)}, f32[48,32,128]{2,1,0:T(8,128)S(1)}, u32[]{:S(2)}, u32[]{:S(2)}) collective-permute-start(f32[48,32,128]{2,1,0:T(8,128)S(1)} %get-tuple-element.135), channel_id=1, source_target_pairs={{0,128},{64,192},{128,0},{192,64},{1,129},{65,193},{129,1},{193,65... | collective-permute-start | bytes 2359304 | tf_op jit(solution)/shard_map/cond/branch_1_fun/ppermute | solution.py:510
  36.1 34.1 %collective-permute-start.2 = (f32[48,32,128]{2,1,0:T(8,128)S(1)}, f32[48,32,128]{2,1,0:T(8,128)S(1)}, u32[]{:S(2)}, u32[]{:S(2)}) collective-permute-start(f32[48,32,128]{2,1,0:T(8,128)S(1)} %get-tuple-element.136), channel_id=1, source_target_pairs={{0,192},{64,0},{128,64},{192,128},{1,193},{65,1},{129,65},{193,129... | collective-permute-start | bytes 2359304 | tf_op jit(solution)/shard_map/cond/branch_1_fun/ppermute | solution.py:510
  71.8 1.3 copy-start.1
  82.2 57.1 %all-to-all-start.1 = ((f32[64,2,32,128]{3,2,1,0:T(8,128)}), f32[64,2,32,128]{3,2,1,0:T(8,128)S(1)}, u32[]{:S(2)}, u32[]{:S(2)}) async-start(f32[64,2,32,128]{3,2,1,0:T(8,128)} %bitcast.73), calls=%async_computation.1 | async-start | bytes 4194304 | tf_op jit(solution)/shard_map/cond/branch_1_fun/all_to_all | solution.py:531
  157.7 56.9 %copy-start.4 = (f32[64,2,32,128]{3,2,1,0:T(8,128)}, f32[64,2,32,128]{3,2,1,0:T(8,128)S(1)}, u32[]{:S(2)}) copy-start(f32[64,2,32,128]{3,2,1,0:T(8,128)S(1)} %get-tuple-element.141) | copy-start | bytes 6291460 | tf_op jit(solution)/shard_map/cond
  214.5 57.2 %all-to-all-start.3 = ((f32[64,2,32,128]{3,2,1,0:T(8,128)}), f32[64,2,32,128]{3,2,1,0:T(8,128)}, u32[]{:S(2)}, u32[]{:S(2)}) async-start(f32[64,2,32,128]{3,2,1,0:T(8,128)} %copy-done.4), calls=%async_computation.3 | async-start | bytes 4194304 | tf_op jit(solution)/shard_map/cond/branch_1_fun/all_to_all | solution.py:531
  222.1 19.7 %collective-permute-start.3 = (f32[48,32,128]{2,1,0:T(8,128)S(1)}, f32[48,32,128]{2,1,0:T(8,128)S(1)}, u32[]{:S(2)}, u32[]{:S(2)}) collective-permute-start(f32[48,32,128]{2,1,0:T(8,128)S(1)} %get-tuple-element.138), channel_id=1, source_target_pairs={{0,192},{64,0},{128,64},{192,128},{1,193},{65,1},{129,65},{193,129... | collective-permute-start | bytes 2359304 | tf_op jit(solution)/shard_map/cond/branch_1_fun/ppermute | solution.py:510
  224.7 19.9 %collective-permute-start.4 = (f32[48,32,128]{2,1,0:T(8,128)S(1)}, f32[48,32,128]{2,1,0:T(8,128)S(1)}, u32[]{:S(2)}, u32[]{:S(2)}) collective-permute-start(f32[48,32,128]{2,1,0:T(8,128)S(1)} %get-tuple-element.139), channel_id=1, source_target_pairs={{0,128},{64,192},{128,0},{192,64},{1,129},{65,193},{129,1},{193,65... | collective-permute-start | bytes 2359304 | tf_op jit(solution)/shard_map/cond/branch_1_fun/ppermute | solution.py:510
  225.2 37.4 %collective-permute-start.5 = (f32[48,32,128]{2,1,0:T(8,128)S(1)}, f32[48,32,128]{2,1,0:T(8,128)S(1)}, u32[]{:S(2)}, u32[]{:S(2)}) collective-permute-start(f32[48,32,128]{2,1,0:T(8,128)S(1)} %get-tuple-element.140), channel_id=1, source_target_pairs={{0,64},{64,128},{128,192},{192,0},{1,65},{65,129},{129,193},{193,1... | collective-permute-start | bytes 2359304 | tf_op jit(solution)/shard_map/cond/branch_1_fun/ppermute | solution.py:510
  267.3 1.3 copy-start.2
  271.7 1.6 copy-start.3
where the time goes:
time: 286 us
  waiting for transfers between devices  133 us (47%)
  blocking collectives  56.9 us (20%)
  Pallas kernels  38.8 us (14%)
  starting transfers between devices  33.7 us (12%)
  between operations  14 us (5%)
  local copies, waits for them, and re-layouts  9.07 us (3%)
    ppermute x6, waiting for transfers between devices, turned(): lax.ppermute(x, 'grp', [(g, (g + shift) % groups) for g in range(groups)])  69.7 us
    all_to_all x3, waiting for transfers between devices, exchanged(): lax.all_to_all(planes.reshape(B, PAIR_DEV, ROWS, 128), 'grid', 0, 0, tile...  63 us
    all_to_all x1, blocking collectives, exchanged(): lax.all_to_all(planes.reshape(B, PAIR_DEV, ROWS, 128), 'grid', 0, 0, tile...  56.9 us
    all_to_all x3, starting transfers between devices, exchanged(): lax.all_to_all(planes.reshape(B, PAIR_DEV, ROWS, 128), 'grid', 0, 0, tile...  25.2 us
    pallas_call x1, Pallas kernels, solve(): pl.pallas_call(pair_kernel, out_shape=[jax.ShapeDtypeStruct((B, PAIR_DEV,...  18.4 us
    ppermute x6, starting transfers between devices, turned(): lax.ppermute(x, 'grp', [(g, (g + shift) % groups) for g in range(groups)])  8.58 us
    cond x11, local copies, waits for them, and re-layouts  7.49 us
  transfers between devices with their start and end apart: 9, of which 8 were waited for; matrix products, arithmetic and copies ran while one was open for 0% of the time, Pallas kernels for 3%

commit v1 on v0

--- a/solution.py
+++ b/solution.py
@@ -12,7 +12,8 @@
 ITERS = 3
 ROWS = B * B // 128
 KEEP = 48
-UNROLL = 8
+UNROLL = 32
+BLOCK = 8
 
 
 def shift_field(field, offset, extent):
@@ -258,49 +259,56 @@
     )(idx, *tables)
 
 
-def solve_pair(orb_a, orb_b, anchor_ref, box_a, box_b, term_a, term_b, part, dens, resid, second, third, image):
-    ox, oy, oz = [anchor_ref[3 * orb_b + k] - anchor_ref[3 * orb_a + k] for k in range(3)]
+def solve_pair(offset, box_a, box_b, term_a, term_b, part, dens, resid, second, third, image):
+    ox, oy, oz = offset
     shape = (ROWS, 128)
     line = lax.broadcasted_iota(jnp.int32, shape, 0)
     lane = lax.broadcasted_iota(jnp.int32, shape, 1)
     cy = 2 * line + (lane >> 6)
-    cz = lane & 63
-    low = lane < 64
-    no_y = ((cy == 0) | (cy == B - 1))
+    cz = lane & (B - 1)
+    high = lane >= B
+    ends = (high & (line == 0)) | (~high & (line == ROWS - 1))
     no_up, no_down = cz == B - 1, cz == 0
 
+    def plane(ref, x):
+        return ref[pl.ds(pl.multiple_of(x * ROWS, ROWS), ROWS)]
+
+    def put(ref, x, value):
+        ref[pl.ds(pl.multiple_of(x * ROWS, ROWS), ROWS)] = value
+
     def shifter(sy, sz):
-        flat = (sy * B + sz + B * B) & (B * B - 1)
+        flat = sy * B + sz
         lines, steps = flat >> 7, flat & 127
         inside = (cy >= sy) & (cy < B + sy) & (cz >= sz) & (cz < B + sz)
-        keep = lane >= steps
-
-        def shift(plane):
-            turned = pltpu.roll(plane, steps, axis=1)
-            turned = jnp.where(keep, turned, pltpu.roll(turned, 1, axis=0))
-            return jnp.where(inside, pltpu.roll(turned, lines, axis=0), 0.0)
+        keep = lane < 128 - steps
+
+        def shift(ref, x):
+            at = x * ROWS - lines
+            moved = jnp.where(keep, ref[pl.ds(at, ROWS)], ref[pl.ds(at - 1, ROWS)])
+            return jnp.where(inside, pltpu.roll(moved, steps, axis=1), 0.0)
 
         return shift
 
     def apply(ref, x):
-        here = ref[x + 1]
-        swapped = pltpu.roll(here, 64, axis=1)
-        other = jnp.where(low, pltpu.roll(swapped, 1, axis=0), pltpu.roll(swapped, ROWS - 1, axis=0))
-        beside = ref[x] + ref[x + 2] + swapped + jnp.where(no_y, 0.0, other)
+        here = plane(ref, x + 1)
+        at = (x + 1) * ROWS
+        other = jnp.where(high, ref[pl.ds(at - 1, ROWS)], ref[pl.ds(at + 1, ROWS)])
+        other = here + jnp.where(ends, 0.0, other)
+        beside = plane(ref, x) + plane(ref, x + 2) + pltpu.roll(other, B, axis=1)
         upper = jnp.where(no_up, 0.0, pltpu.roll(here, 127, axis=1))
         lower = jnp.where(no_down, 0.0, pltpu.roll(here, 1, axis=1))
         return here, 6.0 * here - beside - upper - lower
 
     zero = jnp.zeros(shape, jnp.float32)
     for ref in (dens, second, third):
-        ref[0] = zero
-        ref[B + 1] = zero
+        put(ref, 0, zero)
+        put(ref, B + 1, zero)
 
     def total(x):
         return jnp.sum(x, keepdims=True)
 
-    def planes(step, init=None):
-        return lax.fori_loop(0, B, step, zero if init is None else init, unroll=UNROLL)
+    def planes(step):
+        return lax.fori_loop(0, B, step, zero, unroll=UNROLL)
 
     shift_on = shifter(oy, oz)
     shift_back = shifter(-oy, -oz)
@@ -308,52 +316,52 @@
     def begin(x, acc):
         src = x - ox
         inside = jnp.where((src >= 0) & (src < B), 1.0, 0.0)
-        moved = shift_on(box_b[jnp.clip(src, 0, B - 1)]) * inside
-        density = box_a[x] * moved
-        part[x] = moved
-        dens[x + 1] = density
+        moved = shift_on(box_b, jnp.clip(src, 0, B - 1) + 1) * inside
+        density = plane(box_a, x + 1) * moved
+        put(part, x, moved)
+        put(dens, x + 1, density)
         return acc + density * density
 
     norm0 = total(planes(begin))
 
     def first(x, acc):
         here, img = apply(dens, x)
-        image[x] = img
+        put(image, x + 1, img)
         return acc + here * img
 
     step0 = norm0 / total(planes(first))
 
     def rest0(x, acc):
-        left = dens[x + 1] - step0 * image[x]
-        resid[x] = left
+        left = plane(dens, x + 1) - step0 * plane(image, x + 1)
+        put(resid, x, left)
         return acc + left * left
 
     norm1 = total(planes(rest0))
     ratio0 = norm1 / norm0
 
     def turn1(x, acc):
-        second[x + 1] = resid[x] + ratio0 * dens[x + 1]
+        put(second, x + 1, plane(resid, x) + ratio0 * plane(dens, x + 1))
         return acc
 
     planes(turn1)
 
     def again(x, acc):
         here, img = apply(second, x)
-        image[x] = img
+        put(image, x + 1, img)
         return acc + here * img
 
     step1 = norm1 / total(planes(again))
 
     def rest1(x, acc):
-        left = resid[x] - step1 * image[x]
-        resid[x] = left
+        left = plane(resid, x) - step1 * plane(image, x + 1)
+        put(resid, x, left)
         return acc + left * left
 
     norm2 = total(planes(rest1))
     ratio1 = norm2 / norm1
 
     def turn2(x, acc):
-        third[x + 1] = resid[x] + ratio1 * second[x + 1]
+        put(third, x + 1, plane(resid, x) + ratio1 * plane(second, x + 1))
         return acc
 
     planes(turn2)
@@ -365,9 +373,9 @@
     step2 = norm2 / total(planes(last))
 
     def finish(x, acc):
-        potential = step0 * dens[x + 1] + step1 * second[x + 1] + step2 * third[x + 1]
-        term_a[x] = potential * part[x]
-        image[x] = potential * box_a[x]
+        potential = step0 * plane(dens, x + 1) + step1 * plane(second, x + 1) + step2 * plane(third, x + 1)
+        put(term_a, x, potential * plane(part, x))
+        put(image, x + 1, potential * plane(box_a, x + 1))
         return acc
 
     planes(finish)
@@ -375,7 +383,7 @@
     def back(x, acc):
         src = x + ox
         inside = jnp.where((src >= 0) & (src < B), 1.0, 0.0)
-        term_b[x] = shift_back(image[jnp.clip(src, 0, B - 1)]) * inside
+        put(term_b, x, shift_back(image, jnp.clip(src, 0, B - 1) + 1) * inside)
         return acc
 
     planes(back)
@@ -383,13 +391,17 @@
 
 def pair_kernel(place_ref, pos_ref, anchor_ref, near_ref, far_ref, near_out, far_out, boxes, terms, *rest):
     *fields, sem_in, sem_out = rest
+
+    def flat(ref):
+        return ref.reshape(ref.shape[0] * ROWS, 128)
+
     at = [s * B + place_ref[0] for s in range(PAIR_DEV)]
     flags = [pos_ref[4, k] for k in at]
 
     def pulls(s):
         return [
-            pltpu.make_async_copy(near_ref.at[:, s], boxes.at[s, flags[s]], sem_in.at[s, 0]),
-            pltpu.make_async_copy(far_ref.at[:, s], boxes.at[s, 1 - flags[s]], sem_in.at[s, 1]),
+            pltpu.make_async_copy(near_ref.at[:, s], boxes.at[s, flags[s], pl.ds(1, B)], sem_in.at[s, 0]),
+            pltpu.make_async_copy(far_ref.at[:, s], boxes.at[s, 1 - flags[s], pl.ds(1, B)], sem_in.at[s, 1]),
         ]
 
     def pushes(s):
@@ -404,10 +416,9 @@
     for s in range(PAIR_DEV):
         for copy in pulls(s):
             copy.wait()
-        solve_pair(
-            pos_ref[2, at[s]], pos_ref[3, at[s]], anchor_ref,
-            boxes.at[s, 0], boxes.at[s, 1], terms.at[s, 0], terms.at[s, 1], *fields,
-        )
+        orb_a, orb_b = pos_ref[2, at[s]], pos_ref[3, at[s]]
+        offset = [anchor_ref[3 * orb_b + k] - anchor_ref[3 * orb_a + k] for k in range(3)]
+        solve_pair(offset, *[flat(ref.at[s, k]) for ref in (boxes, terms) for k in range(2)], *fields)
         for copy in pushes(s):
             copy.start()
     for s in range(PAIR_DEV):
@@ -418,16 +429,17 @@
 def solve(place, pos, anchors, near, far):
     smem = pl.BlockSpec(memory_space=pltpu.SMEM)
     anywhere = pl.BlockSpec(memory_space=pl.ANY)
-    field = pltpu.VMEM((B, ROWS, 128), jnp.float32)
-    padded = pltpu.VMEM((B + 2, ROWS, 128), jnp.float32)
-    two = pltpu.VMEM((PAIR_DEV, 2, B, ROWS, 128), jnp.float32)
+    field = pltpu.VMEM((B * ROWS, 128), jnp.float32)
+    padded = pltpu.VMEM(((B + 2) * ROWS, 128), jnp.float32)
+    boxes = pltpu.VMEM((PAIR_DEV, 2, B + 2, ROWS, 128), jnp.float32)
+    terms = pltpu.VMEM((PAIR_DEV, 2, B, ROWS, 128), jnp.float32)
     dma = pltpu.SemaphoreType.DMA((PAIR_DEV, 2))
     return pl.pallas_call(
         pair_kernel,
         out_shape=[jax.ShapeDtypeStruct((B, PAIR_DEV, ROWS, 128), jnp.float32)] * 2,
         in_specs=[smem, smem, smem, anywhere, anywhere],
         out_specs=[anywhere, anywhere],
-        scratch_shapes=[two, two, field, padded, field, padded, padded, field, dma, dma],
+        scratch_shapes=[boxes, terms, field, padded, field, padded, padded, padded, dma, dma],
         compiler_params=pltpu.CompilerParams(vmem_limit_bytes=32 << 20),
         cost_estimate=pl.CostEstimate(flops=100_000_000, bytes_accessed=30_000_000, transcendentals=0),
         name="solve",
@@ -486,34 +498,65 @@
             acc[j] = acc[j] + terms_ref[p, s]
         return carry
 
-    lax.fori_loop(0, B, here, 0)
-    for j in range(ROWS):
+    lax.fori_loop(0, B, here, 0, unroll=4)
+    for j in range(BLOCK):
         out_ref[:, j * 128 : (j + 1) * 128] = acc[:, j, :]
 
 
 def add_near(pos, summed, terms):
-    smem, vmem = pl.BlockSpec(memory_space=pltpu.SMEM), pl.BlockSpec(memory_space=pltpu.VMEM)
     return pl.pallas_call(
         add_near_kernel,
         out_shape=jax.ShapeDtypeStruct((128, ROWS * 128), jnp.float32),
-        in_specs=[smem, vmem, vmem],
-        out_specs=vmem,
-        scratch_shapes=[pltpu.VMEM((128, ROWS, 128), jnp.float32)],
-        compiler_params=pltpu.CompilerParams(vmem_limit_bytes=24 << 20),
+        grid=(ROWS // BLOCK,),
+        in_specs=[
+            pl.BlockSpec(memory_space=pltpu.SMEM),
+            pl.BlockSpec((128, BLOCK, 128), lambda i: (0, i, 0)),
+            pl.BlockSpec((B, PAIR_DEV, BLOCK, 128), lambda i: (0, 0, i, 0)),
+        ],
+        out_specs=pl.BlockSpec((128, BLOCK * 128), lambda i: (0, i)),
+        scratch_shapes=[pltpu.VMEM((128, BLOCK, 128), jnp.float32)],
+        compiler_params=pltpu.CompilerParams(vmem_limit_bytes=60 << 20),
         cost_estimate=pl.CostEstimate(flops=2_000_000, bytes_accessed=10_000_000, transcendentals=0),
         name="add_near",
     )(pos, summed, terms)
 
 
+def deal_near_kernel(pos_ref, orb_ref, local_ref, near_ref, table):
+    for j in range(BLOCK):
+        table[:, j, :] = orb_ref[:, j * 128 : (j + 1) * 128]
+    local_ref[...] = table[...]
+
+    def here(p, carry):
+        for s in range(PAIR_DEV):
+            near_ref[p, s] = table[pos_ref[0, s * B + p]]
+        return carry
+
+    lax.fori_loop(0, B, here, 0, unroll=4)
+
+
+def deal_near(pos, orbitals):
+    rows = pl.BlockSpec((128, BLOCK, 128), lambda i: (0, i, 0))
+    return pl.pallas_call(
+        deal_near_kernel,
+        out_shape=[
+            jax.ShapeDtypeStruct((128, ROWS, 128), jnp.float32),
+            jax.ShapeDtypeStruct((B, PAIR_DEV, ROWS, 128), jnp.float32),
+        ],
+        grid=(ROWS // BLOCK,),
+        in_specs=[pl.BlockSpec(memory_space=pltpu.SMEM), pl.BlockSpec((128, BLOCK * 128), lambda i: (0, i))],
+        out_specs=[rows, pl.BlockSpec((B, PAIR_DEV, BLOCK, 128), lambda i: (0, 0, i, 0))],
+        scratch_shapes=[pltpu.VMEM((128, BLOCK, 128), jnp.float32)],
+        compiler_params=pltpu.CompilerParams(vmem_limit_bytes=60 << 20),
+        cost_estimate=pl.CostEstimate(flops=2_000_000, bytes_accessed=10_000_000, transcendentals=0),
+        name="deal_near",
+    )(pos, orbitals)
+
+
 def turned(x, shift):
     groups = lax.axis_size("grp")
     return lax.ppermute(x, "grp", [(g, (g + shift) % groups) for g in range(groups)])
 
 
-def near_row(pos, first, i):
-    return pos[0, (i & 1) * B + (i >> 1)]
-
-
 def far_row(pos, first, i):
     return pos[1, (i & 1) * B + (i >> 1)]
 
@@ -532,8 +575,8 @@
 
 
 def fitting(orbitals, anchors, place, pos, slot):
-    local = orbitals.reshape(128, ROWS, 128)
-    near = exchanged(*fetch(pos, [local], 1, 2 * B, near_row, 0, "deal_near"))
+    local, near = deal_near(pos, orbitals)
+    near = exchanged(near)
     sent = fetch(slot, [local], 3, KEEP, sent_row, 0, "send")
     arrived = [turned(x, d) for d, x in enumerate(sent, 1)]
     far = exchanged(*fetch(pos, [local] + arrived, 1, 2 * B, far_row, 0, "deal_far"))

time: 286 us -> 282 us (0.986)
    pallas_call x1, Pallas kernels: 18.4 us -> 13.6 us  [solve(): pl.pallas_call(pair_kernel, out_shape=[jax.ShapeDtypeStruct((B, PAIR_DEV,...]
    pallas_call x0 -> x1, Pallas kernels: none -> 4.47 us  [deal_near(): pl.pallas_call(deal_near_kernel, out_shape=[jax.ShapeDtypeStruct((128, RO...]
    cond x11 -> x8, local copies, waits for them, and re-layouts: 7.49 us -> 4.22 us
where the time goes in v1:
time: 282 us; the launch traced here: 281 us
  waiting for transfers between devices  131 us (46%)
  blocking collectives  56.9 us (20%)
  Pallas kernels  37.4 us (13%)
  starting transfers between devices  33.7 us (12%)
  between operations  14 us (5%)
  local copies, waits for them, and re-layouts  7.87 us (3%)
    ppermute x6, waiting for transfers between devices, turned(): lax.ppermute(x, 'grp', [(g, (g + shift) % groups) for g in range(groups)])  69.7 us
    all_to_all x3, waiting for transfers between devices, exchanged(): lax.all_to_all(planes.reshape(B, PAIR_DEV, ROWS, 128), 'grid', 0, 0, tile...  61.5 us
    all_to_all x1, blocking collectives, exchanged(): lax.all_to_all(planes.reshape(B, PAIR_DEV, ROWS, 128), 'grid', 0, 0, tile...  56.9 us
    all_to_all x3, starting transfers between devices, exchanged(): lax.all_to_all(planes.reshape(B, PAIR_DEV, ROWS, 128), 'grid', 0, 0, tile...  25.2 us
    pallas_call x1, Pallas kernels, solve(): pl.pallas_call(pair_kernel, out_shape=[jax.ShapeDtypeStruct((B, PAIR_DEV,...  13.6 us
    ppermute x6, starting transfers between devices, turned(): lax.ppermute(x, 'grp', [(g, (g + shift) % groups) for g in range(groups)])  8.55 us
  transfers between devices with their start and end apart: 9, of which 8 were waited for; matrix products, arithmetic and copies ran while one was open for 0% of the time, Pallas kernels for 3%

profile of v1, /device:TPU:1, one launch (start us, length us, event | category | flops | bytes accessed | tf_op | source)
XLA Modules:
  0.0 281.5 jit_solution(11891391076798402005)
XLA Ops:
  6.5 1.9 copy.32
  9.8 4.6 %route.1 = (s32[8,128]{1,0:T(8,128)S(1)}, s32[8,256]{1,0:T(8,128)S(1)}, s32[1]{0:T(128)}) custom-call(s32[1]{0:T(128)} %bitcast.20.me_ref, s32[1024,1]{1,0:T(8,128)S(1)} %get-tuple-element.243.a_ref, s32[1024,1]{1,0:T(8,128)S(1)} %get-tuple-element.242.b_ref), custom_call_target="tpu_custom_call" | custom-call | flops 10000000 | bytes 1000000 | tf_op jit(solution)/shard_map/route/pallas_call | solution.py:213
  15.1 259.6 %conditional.1 = (f32[128,4096]{1,0:T(8,128)}) conditional(s32[]{:T(128)} %bitcast.22, (s32[256,4,2]{0,2,1:T(2,128)S(1)}, f32[128,4096]{1,0:T(8,128)S(1)}, s32[512,3]{0,1:T(4,128)S(1)}) %tuple.95, (s32[]{:T(128)}, s32[512,3]{0,1:T(4,128)S(1)}, s32[8,128]{1,0:T(8,128)S(1)}, f32[128,4096]{1,0:T(8,128)S(1)}, s32[8,256]{1,0:T(8,128)S(1)}) %tuple.96), branch_computations={%region_0.12_spmd, %region_12.13_spmd} | conditional | flops 106000000 | bytes 194176512 | solution.py:595
  15.3 4.5 %deal_near.1 = (f32[128,32,128]{2,1,0:T(8,128)}, f32[64,2,32,128]{3,2,1,0:T(8,128)}) custom-call(s32[8,128]{1,0:T(8,128)S(1)} %get-tuple-element.130.pos_ref.idx_ref, f32[128,4096]{1,0:T(8,128)S(1)} %get-tuple-element.134.orb_ref), custom_call_target="tpu_custom_call" | custom-call | flops 2000000 | bytes 10000000 | tf_op jit(solution)/shard_map/cond/branch_1_fun/deal_near/pallas_call | solution.py:539
  19.8 13.2 %all-to-all-start = ((f32[64,2,32,128]{3,2,1,0:T(8,128)}), f32[64,2,32,128]{3,2,1,0:T(8,128)S(1)}, u32[]{:S(2)}, u32[]{:S(2)}) async-start(f32[64,2,32,128]{3,2,1,0:T(8,128)} %get-tuple-element.135), calls=%async_computation | async-start | bytes 4194304 | tf_op jit(solution)/shard_map/cond/branch_1_fun/all_to_all | solution.py:574
  33.0 1.6 copy-done
  37.2 2.4 collective-permute-start.1
  40.8 15.1 %collective-permute-done.refs_1_ = f32[48,32,128]{2,1,0:T(8,128)S(1)} collective-permute-done((f32[48,32,128]{2,1,0:T(8,128)S(1)}, f32[48,32,128]{2,1,0:T(8,128)S(1)}, u32[]{:S(2)}, u32[]{:S(2)}) %collective-permute-start) | collective-permute-done | bytes 786464 | tf_op jit(solution)/shard_map/cond/branch_1_fun/ppermute | solution.py:557
  55.8 17.8 %collective-permute-done.1.refs_2_ = f32[48,32,128]{2,1,0:T(8,128)S(1)} collective-permute-done((f32[48,32,128]{2,1,0:T(8,128)S(1)}, f32[48,32,128]{2,1,0:T(8,128)S(1)}, u32[]{:S(2)}, u32[]{:S(2)}) %collective-permute-start.1) | collective-permute-done | bytes 786464 | tf_op jit(solution)/shard_map/cond/branch_1_fun/ppermute | solution.py:557
  73.7 1.6 deal_far.1
  76.6 7.6 %all-to-all-done.near_ref = f32[64,2,32,128]{3,2,1,0:T(8,128)S(1)} async-done(((f32[64,2,32,128]{3,2,1,0:T(8,128)}), f32[64,2,32,128]{3,2,1,0:T(8,128)S(1)}, u32[]{:S(2)}, u32[]{:S(2)}) %all-to-all-start) | async-done | bytes 2097184 | tf_op jit(solution)/shard_map/cond/branch_1_fun/all_to_all | solution.py:574
  84.2 6.0 %all-to-all-start.1 = ((f32[64,2,32,128]{3,2,1,0:T(8,128)}), f32[64,2,32,128]{3,2,1,0:T(8,128)}, u32[]{:S(2)}, u32[]{:S(2)}) async-start(f32[64,2,32,128]{3,2,1,0:T(8,128)} %bitcast.66), calls=%async_computation.1 | async-start | bytes 4194304 | tf_op jit(solution)/shard_map/cond/branch_1_fun/all_to_all | solution.py:574
  90.6 50.8 %all-to-all-done.1.far_ref = f32[64,2,32,128]{3,2,1,0:T(8,128)} async-done(((f32[64,2,32,128]{3,2,1,0:T(8,128)}), f32[64,2,32,128]{3,2,1,0:T(8,128)}, u32[]{:S(2)}, u32[]{:S(2)}) %all-to-all-start.1) | async-done | bytes 2097184 | tf_op jit(solution)/shard_map/cond/branch_1_fun/all_to_all | solution.py:574
  141.4 13.6 %solve.1 = (f32[64,2,32,128]{3,2,1,0:T(8,128)S(1)}, f32[64,2,32,128]{3,2,1,0:T(8,128)S(1)}) custom-call(s32[1]{0:T(128)} %bitcast.17.place_ref, s32[8,128]{1,0:T(8,128)S(1)} %get-tuple-element.130.pos_ref.idx_ref, s32[1536]{0:T(1024)S(1)} %reshape.240.anchor_ref, f32[64,2,32,128]{3,2,1,0:T(8,128)S(1)} %all-to-all-done.near_ref, ...), custom_call_target="tpu_custom_call" | custom-call | flops 100000000 | bytes 30000000 | tf_op jit(solution)/shard_map/cond/branch_1_fun/solve/pallas_call | solution.py:437
  155.0 56.9 %all_to_all.24.terms_ref = f32[64,2,32,128]{3,2,1,0:T(8,128)S(1)} all-to-all(f32[64,2,32,128]{3,2,1,0:T(8,128)S(1)} %get-tuple-element.140), channel_id=1, replica_groups=mesh['grp'=4,'grid'=64] {'grid'}, dimensions={0} | all-to-all | bytes 4194304 | tf_op jit(solution)/shard_map/cond/branch_1_fun/all_to_all | solution.py:574
  211.8 6.0 %all-to-all-start.3 = ((f32[64,2,32,128]{3,2,1,0:T(8,128)}), f32[64,2,32,128]{3,2,1,0:T(8,128)}, u32[]{:S(2)}, u32[]{:S(2)}) async-start(f32[64,2,32,128]{3,2,1,0:T(8,128)} %copy-done.3), calls=%async_computation.3 | async-start | bytes 4194304 | tf_op jit(solution)/shard_map/cond/branch_1_fun/all_to_all | solution.py:574
  217.9 1.5 back.1
  219.4 2.6 collective-permute-start.3
  223.1 16.1 %collective-permute-done.3.refs_0_ = f32[48,32,128]{2,1,0:T(8,128)S(1)} collective-permute-done((f32[48,32,128]{2,1,0:T(8,128)S(1)}, f32[48,32,128]{2,1,0:T(8,128)S(1)}, u32[]{:S(2)}, u32[]{:S(2)}) %collective-permute-start.3) | collective-permute-done | bytes 786464 | tf_op jit(solution)/shard_map/cond/branch_1_fun/ppermute | solution.py:557
  239.2 2.7 collective-permute-done.4.refs_1_
  241.9 18.0 %collective-permute-done.5.refs_2_ = f32[48,32,128]{2,1,0:T(8,128)S(1)} collective-permute-done((f32[48,32,128]{2,1,0:T(8,128)S(1)}, f32[48,32,128]{2,1,0:T(8,128)S(1)}, u32[]{:S(2)}, u32[]{:S(2)}) %collective-permute-start.5) | collective-permute-done | bytes 786464 | tf_op jit(solution)/shard_map/cond/branch_1_fun/ppermute | solution.py:557
  259.9 4.7 %add_far.1.sum_ref = f32[128,32,128]{2,1,0:T(8,128)S(1)} custom-call(s32[8,128]{1,0:T(8,128)S(1)} %get-tuple-element.130.pos_ref.idx_ref, s32[8,256]{1,0:T(8,128)S(1)} %get-tuple-element.131.idx_ref.slot_ref, f32[64,2,32,128]{3,2,1,0:T(8,128)S(1)} %all_to_all.24.terms_ref, f32[48,32,128]{2,1,0:T(8,128)S(1)} %collective-permute-done.3.refs_0_, ...), custom_call_target="tpu_custom_call" | custom-call | flops 2000000 | bytes 10000000 | tf_op jit(solution)/shard_map/cond/branch_1_fun/add_far/pallas_call | solution.py:481
  265.9 3.1 %all-to-all-done.3.terms_ref = f32[64,2,32,128]{3,2,1,0:T(8,128)} async-done(((f32[64,2,32,128]{3,2,1,0:T(8,128)}), f32[64,2,32,128]{3,2,1,0:T(8,128)}, u32[]{:S(2)}, u32[]{:S(2)}) %all-to-all-start.3) | async-done | bytes 2097184 | tf_op jit(solution)/shard_map/cond/branch_1_fun/all_to_all | solution.py:574
  269.0 5.6 %add_near.1 = f32[128,4096]{1,0:T(8,128)} custom-call(s32[8,128]{1,0:T(8,128)S(1)} %get-tuple-element.130.pos_ref.idx_ref, f32[128,32,128]{2,1,0:T(8,128)} %copy-done.2, f32[64,2,32,128]{3,2,1,0:T(8,128)} %all-to-all-done.3.terms_ref), custom_call_target="tpu_custom_call" | custom-call | flops 2000000 | bytes 10000000 | tf_op jit(solution)/shard_map/cond/branch_1_fun/add_near/pallas_call | solution.py:507
  (22 shorter events, 9.3 us)
Async XLA Ops:
  6.5 8.5 %copy-start.9 = (s32[256,4,2]{0,2,1:T(2,128)S(1)}, s32[256,4,2]{0,2,1:T(2,128)}, u32[]{:S(2)}) copy-start(s32[256,4,2]{0,2,1:T(2,128)} %param.9) | copy-start | bytes 24580
  6.5 8.5 %copy-start.7 = (f32[128,4096]{1,0:T(8,128)S(1)}, f32[128,4096]{1,0:T(8,128)}, u32[]{:S(2)}) copy-start(f32[128,4096]{1,0:T(8,128)} %param.7) | copy-start | bytes 6291460
  6.5 8.5 %copy-start.10 = (s32[512,3]{0,1:T(4,128)S(1)}, s32[512,3]{0,1:T(4,128)}, u32[]{:S(2)}) copy-start(s32[512,3]{0,1:T(4,128)} %param.8) | copy-start | bytes 18436
  19.8 64.4 %all-to-all-start = ((f32[64,2,32,128]{3,2,1,0:T(8,128)}), f32[64,2,32,128]{3,2,1,0:T(8,128)S(1)}, u32[]{:S(2)}, u32[]{:S(2)}) async-start(f32[64,2,32,128]{3,2,1,0:T(8,128)} %get-tuple-element.135), calls=%async_computation | async-start | bytes 4194304 | tf_op jit(solution)/shard_map/cond/branch_1_fun/all_to_all | solution.py:574
  32.9 1.6 copy-start
  35.9 19.9 %collective-permute-start = (f32[48,32,128]{2,1,0:T(8,128)S(1)}, f32[48,32,128]{2,1,0:T(8,128)S(1)}, u32[]{:S(2)}, u32[]{:S(2)}) collective-permute-start(f32[48,32,128]{2,1,0:T(8,128)S(1)} %get-tuple-element.137), channel_id=1, source_target_pairs={{0,64},{64,128},{128,192},{192,0},{1,65},{65,129},{129,193},{193,1... | collective-permute-start | bytes 2359304 | tf_op jit(solution)/shard_map/cond/branch_1_fun/ppermute | solution.py:557
  37.2 36.5 %collective-permute-start.1 = (f32[48,32,128]{2,1,0:T(8,128)S(1)}, f32[48,32,128]{2,1,0:T(8,128)S(1)}, u32[]{:S(2)}, u32[]{:S(2)}) collective-permute-start(f32[48,32,128]{2,1,0:T(8,128)S(1)} %get-tuple-element.138), channel_id=1, source_target_pairs={{0,128},{64,192},{128,0},{192,64},{1,129},{65,193},{129,1},{193,65... | collective-permute-start | bytes 2359304 | tf_op jit(solution)/shard_map/cond/branch_1_fun/ppermute | solution.py:557
  39.6 34.1 %collective-permute-start.2 = (f32[48,32,128]{2,1,0:T(8,128)S(1)}, f32[48,32,128]{2,1,0:T(8,128)S(1)}, u32[]{:S(2)}, u32[]{:S(2)}) collective-permute-start(f32[48,32,128]{2,1,0:T(8,128)S(1)} %get-tuple-element.139), channel_id=1, source_target_pairs={{0,192},{64,0},{128,64},{192,128},{1,193},{65,1},{129,65},{193,129... | collective-permute-start | bytes 2359304 | tf_op jit(solution)/shard_map/cond/branch_1_fun/ppermute | solution.py:557
  75.3 1.3 copy-start.1
  84.2 57.2 %all-to-all-start.1 = ((f32[64,2,32,128]{3,2,1,0:T(8,128)}), f32[64,2,32,128]{3,2,1,0:T(8,128)}, u32[]{:S(2)}, u32[]{:S(2)}) async-start(f32[64,2,32,128]{3,2,1,0:T(8,128)} %bitcast.66), calls=%async_computation.1 | async-start | bytes 4194304 | tf_op jit(solution)/shard_map/cond/branch_1_fun/all_to_all | solution.py:574
  155.0 56.9 %copy-start.3 = (f32[64,2,32,128]{3,2,1,0:T(8,128)}, f32[64,2,32,128]{3,2,1,0:T(8,128)S(1)}, u32[]{:S(2)}) copy-start(f32[64,2,32,128]{3,2,1,0:T(8,128)S(1)} %get-tuple-element.144) | copy-start | bytes 6291460 | tf_op jit(solution)/shard_map/cond
  211.8 57.2 %all-to-all-start.3 = ((f32[64,2,32,128]{3,2,1,0:T(8,128)}), f32[64,2,32,128]{3,2,1,0:T(8,128)}, u32[]{:S(2)}, u32[]{:S(2)}) async-start(f32[64,2,32,128]{3,2,1,0:T(8,128)} %copy-done.3), calls=%async_computation.3 | async-start | bytes 4194304 | tf_op jit(solution)/shard_map/cond/branch_1_fun/all_to_all | solution.py:574
  219.4 19.8 %collective-permute-start.3 = (f32[48,32,128]{2,1,0:T(8,128)S(1)}, f32[48,32,128]{2,1,0:T(8,128)S(1)}, u32[]{:S(2)}, u32[]{:S(2)}) collective-permute-start(f32[48,32,128]{2,1,0:T(8,128)S(1)} %get-tuple-element.141), channel_id=1, source_target_pairs={{0,192},{64,0},{128,64},{192,128},{1,193},{65,1},{129,65},{193,129... | collective-permute-start | bytes 2359304 | tf_op jit(solution)/shard_map/cond/branch_1_fun/ppermute | solution.py:557
  222.0 19.9 %collective-permute-start.4 = (f32[48,32,128]{2,1,0:T(8,128)S(1)}, f32[48,32,128]{2,1,0:T(8,128)S(1)}, u32[]{:S(2)}, u32[]{:S(2)}) collective-permute-start(f32[48,32,128]{2,1,0:T(8,128)S(1)} %get-tuple-element.142), channel_id=1, source_target_pairs={{0,128},{64,192},{128,0},{192,64},{1,129},{65,193},{129,1},{193,65... | collective-permute-start | bytes 2359304 | tf_op jit(solution)/shard_map/cond/branch_1_fun/ppermute | solution.py:557
  222.5 37.4 %collective-permute-start.5 = (f32[48,32,128]{2,1,0:T(8,128)S(1)}, f32[48,32,128]{2,1,0:T(8,128)S(1)}, u32[]{:S(2)}, u32[]{:S(2)}) collective-permute-start(f32[48,32,128]{2,1,0:T(8,128)S(1)} %get-tuple-element.143), channel_id=1, source_target_pairs={{0,64},{64,128},{128,192},{192,0},{1,65},{65,129},{129,193},{193,1... | collective-permute-start | bytes 2359304 | tf_op jit(solution)/shard_map/cond/branch_1_fun/ppermute | solution.py:557
  264.6 1.3 copy-start.2

commit v2 on v1

--- a/solution.py
+++ b/solution.py
@@ -12,8 +12,7 @@
 ITERS = 3
 ROWS = B * B // 128
 KEEP = 48
-UNROLL = 32
-BLOCK = 8
+UNROLL = 16
 
 
 def shift_field(field, offset, extent):
@@ -111,21 +110,32 @@
     return lax.psum_scatter(summed, "grp", scatter_dimension=0, tiled=True)
 
 
-def route_kernel(me_ref, a_ref, b_ref, pos_ref, slot_ref, fits_ref):
+def route_kernel(me_ref, pair_ref, pos_ref, slot_ref, fits_ref):
     me = me_ref[0]
-    a, b = a_ref[...], b_ref[...]
-    n = a.shape[0]
     f32, i32 = jnp.float32, jnp.int32
     groups, each = 4, 2 * B
 
     def col(x):
         return jnp.sum(x, axis=1, keepdims=True)
 
-    before = lax.broadcasted_iota(i32, (n, n), 0) > lax.broadcasted_iota(i32, (n, n), 1)
+    pairs = pair_ref[...].astype(f32).T
+    at = lax.broadcasted_iota(i32, pairs.shape, 1)
+    columns = [col(jnp.where(at == k, pairs, 0.0)) for k in range(pairs.shape[1])]
+    a = jnp.concatenate(columns[0::2], axis=0).astype(i32)
+    b = jnp.concatenate(columns[1::2], axis=0).astype(i32)
+    n = a.shape[0]
+
+    before = lax.broadcasted_iota(i32, (128, 128), 0) > lax.broadcasted_iota(i32, (128, 128), 1)
     before = jnp.where(before, 1.0, 0.0).astype(jnp.bfloat16)
 
     def rank_in(hot):
-        return col(jnp.dot(before, hot.astype(jnp.bfloat16), preferred_element_type=f32) * hot).astype(i32)
+        ranks, passed = [], jnp.zeros((1, 128), f32)
+        for k in range(0, n, 128):
+            part = hot[k : k + 128]
+            ahead = jnp.dot(before, part.astype(jnp.bfloat16), preferred_element_type=f32) + passed
+            ranks.append(col(ahead * part))
+            passed = passed + jnp.sum(part, axis=0, keepdims=True)
+        return jnp.concatenate(ranks, axis=0).astype(i32)
 
     lane = lax.broadcasted_iota(i32, (n, 128), 1)
     valid = a >= 0
@@ -207,7 +217,7 @@
 
 
 def route(me, pair_slots):
-    flat = pair_slots.reshape(-1, 2)
+    lists = jnp.transpose(pair_slots, (1, 2, 0)).reshape(-1, pair_slots.shape[0])
     width = 128 * -(-(3 * KEEP) // 128)
     vmem, smem = pl.BlockSpec(memory_space=pltpu.VMEM), pl.BlockSpec(memory_space=pltpu.SMEM)
     return pl.pallas_call(
@@ -217,12 +227,12 @@
             jax.ShapeDtypeStruct((8, width), jnp.int32),
             jax.ShapeDtypeStruct((1,), jnp.int32),
         ],
-        in_specs=[smem, vmem, vmem],
+        in_specs=[smem, vmem],
         out_specs=[vmem, vmem, smem],
         compiler_params=pltpu.CompilerParams(vmem_limit_bytes=40 << 20),
         cost_estimate=pl.CostEstimate(flops=10_000_000, bytes_accessed=1_000_000, transcendentals=0),
         name="route",
-    )(me, flat[:, :1], flat[:, 1:])
+    )(me, lists)
 
 
 def fetch_kernel(row_of, first, tables, idx_ref, *refs):
@@ -304,12 +314,6 @@
         put(ref, 0, zero)
         put(ref, B + 1, zero)
 
-    def total(x):
-        return jnp.sum(x, keepdims=True)
-
-    def planes(step):
-        return lax.fori_loop(0, B, step, zero, unroll=UNROLL)
-
     shift_on = shifter(oy, oz)
     shift_back = shifter(-oy, -oz)
 
@@ -322,55 +326,52 @@
         put(dens, x + 1, density)
         return acc + density * density
 
-    norm0 = total(planes(begin))
-
     def first(x, acc):
         here, img = apply(dens, x)
         put(image, x + 1, img)
         return acc + here * img
 
-    step0 = norm0 / total(planes(first))
+    norm0 = yield begin
+    step0 = norm0 / (yield first)
 
     def rest0(x, acc):
         left = plane(dens, x + 1) - step0 * plane(image, x + 1)
         put(resid, x, left)
         return acc + left * left
 
-    norm1 = total(planes(rest0))
+    norm1 = yield rest0
     ratio0 = norm1 / norm0
 
     def turn1(x, acc):
         put(second, x + 1, plane(resid, x) + ratio0 * plane(dens, x + 1))
         return acc
-
-    planes(turn1)
 
     def again(x, acc):
         here, img = apply(second, x)
         put(image, x + 1, img)
         return acc + here * img
 
-    step1 = norm1 / total(planes(again))
+    yield turn1
+    step1 = norm1 / (yield again)
 
     def rest1(x, acc):
         left = plane(resid, x) - step1 * plane(image, x + 1)
         put(resid, x, left)
         return acc + left * left
 
-    norm2 = total(planes(rest1))
+    norm2 = yield rest1
     ratio1 = norm2 / norm1
 
     def turn2(x, acc):
         put(third, x + 1, plane(resid, x) + ratio1 * plane(second, x + 1))
         return acc
 
-    planes(turn2)
-
     def last(x, acc):
         here, img = apply(third, x)
         return acc + here * img
 
-    step2 = norm2 / total(planes(last))
+    yield turn2
+    step2 = norm2 / (yield last)
 
     def finish(x, acc):
         potential = step0 * plane(dens, x + 1) + step1 * plane(second, x + 1) + step2 * plane(third, x + 1)
@@ -378,15 +379,29 @@
         put(image, x + 1, potential * plane(box_a, x + 1))
         return acc
 
-    planes(finish)
-
     def back(x, acc):
         src = x + ox
         inside = jnp.where((src >= 0) & (src < B), 1.0, 0.0)
         put(term_b, x, shift_back(image, jnp.clip(src, 0, B - 1) + 1) * inside)
         return acc
 
-    planes(back)
+    yield finish
+    yield back
+
+
+def run_together(solvers):
+    steps = [next(solver) for solver in solvers]
+    zero = jnp.zeros((ROWS, 128), jnp.float32)
+    while True:
+        def both(x, accs, steps=tuple(steps)):
+            return tuple(step(x, acc) for step, acc in zip(steps, accs))
+
+        accs = lax.fori_loop(0, B, both, (zero,) * len(steps), unroll=UNROLL)
+        sums = [jnp.sum(acc, keepdims=True) for acc in accs]
+        try:
+            steps = [solver.send(value) for solver, value in zip(solvers, sums)]
+        except StopIteration:
+            return
 
 
 def pair_kernel(place_ref, pos_ref, anchor_ref, near_ref, far_ref, near_out, far_out, boxes, terms, *rest):
@@ -413,12 +428,16 @@
     for s in range(PAIR_DEV):
         for copy in pulls(s):
             copy.start()
+    solvers = []
     for s in range(PAIR_DEV):
         for copy in pulls(s):
             copy.wait()
         orb_a, orb_b = pos_ref[2, at[s]], pos_ref[3, at[s]]
         offset = [anchor_ref[3 * orb_b + k] - anchor_ref[3 * orb_a + k] for k in range(3)]
-        solve_pair(offset, *[flat(ref.at[s, k]) for ref in (boxes, terms) for k in range(2)], *fields)
+        refs = [flat(ref.at[s, k]) for ref in (boxes, terms) for k in range(2)]
+        solvers.append(solve_pair(offset, *refs, *[ref.at[s] for ref in fields]))
+    run_together(solvers)
+    for s in range(PAIR_DEV):
         for copy in pushes(s):
             copy.start()
     for s in range(PAIR_DEV):
@@ -429,8 +448,8 @@
 def solve(place, pos, anchors, near, far):
     smem = pl.BlockSpec(memory_space=pltpu.SMEM)
     anywhere = pl.BlockSpec(memory_space=pl.ANY)
-    field = pltpu.VMEM((B * ROWS, 128), jnp.float32)
-    padded = pltpu.VMEM(((B + 2) * ROWS, 128), jnp.float32)
+    field = pltpu.VMEM((PAIR_DEV, B * ROWS, 128), jnp.float32)
+    padded = pltpu.VMEM((PAIR_DEV, (B + 2) * ROWS, 128), jnp.float32)
     boxes = pltpu.VMEM((PAIR_DEV, 2, B + 2, ROWS, 128), jnp.float32)
     terms = pltpu.VMEM((PAIR_DEV, 2, B, ROWS, 128), jnp.float32)
     dma = pltpu.SemaphoreType.DMA((PAIR_DEV, 2))
@@ -489,42 +508,46 @@
     )(pos, slot, terms, *from_groups)
 
 
-def add_near_kernel(pos_ref, sum_ref, terms_ref, out_ref, acc):
-    acc[...] = sum_ref[...]
+def add_near_kernel(pos_ref, sum_ref, terms_ref, out_ref, terms, first, second, sem):
+    copies = [
+        pltpu.make_async_copy(terms_ref, terms, sem.at[0]),
+        pltpu.make_async_copy(sum_ref, first, sem.at[1]),
+    ]
+    for copy in copies:
+        copy.start()
+    second[...] = jnp.zeros(second.shape, jnp.float32)
+    for copy in copies:
+        copy.wait()
 
     def here(p, carry):
-        for s in range(PAIR_DEV):
+        for s, total in enumerate((first, second)):
             j = pos_ref[0, s * B + p]
-            acc[j] = acc[j] + terms_ref[p, s]
+            total[j] = total[j] + terms[p, s]
         return carry
 
     lax.fori_loop(0, B, here, 0, unroll=4)
-    for j in range(BLOCK):
-        out_ref[:, j * 128 : (j + 1) * 128] = acc[:, j, :]
+    for j in range(ROWS):
+        out_ref[:, j * 128 : (j + 1) * 128] = first[:, j, :] + second[:, j, :]
 
 
 def add_near(pos, summed, terms):
+    anywhere = pl.BlockSpec(memory_space=pl.ANY)
+    total = pltpu.VMEM((128, ROWS, 128), jnp.float32)
     return pl.pallas_call(
         add_near_kernel,
         out_shape=jax.ShapeDtypeStruct((128, ROWS * 128), jnp.float32),
-        grid=(ROWS // BLOCK,),
-        in_specs=[
-            pl.BlockSpec(memory_space=pltpu.SMEM),
-            pl.BlockSpec((128, BLOCK, 128), lambda i: (0, i, 0)),
-            pl.BlockSpec((B, PAIR_DEV, BLOCK, 128), lambda i: (0, 0, i, 0)),
-        ],
-        out_specs=pl.BlockSpec((128, BLOCK * 128), lambda i: (0, i)),
-        scratch_shapes=[pltpu.VMEM((128, BLOCK, 128), jnp.float32)],
-        compiler_params=pltpu.CompilerParams(vmem_limit_bytes=60 << 20),
+        in_specs=[pl.BlockSpec(memory_space=pltpu.SMEM), anywhere, anywhere],
+        out_specs=pl.BlockSpec(memory_space=pltpu.VMEM),
+        scratch_shapes=[pltpu.VMEM((B, PAIR_DEV, ROWS, 128), jnp.float32), total, total, pltpu.SemaphoreType.DMA((2,))],
+        compiler_params=pltpu.CompilerParams(vmem_limit_bytes=24 << 20),
         cost_estimate=pl.CostEstimate(flops=2_000_000, bytes_accessed=10_000_000, transcendentals=0),
         name="add_near",
     )(pos, summed, terms)
 
 
-def deal_near_kernel(pos_ref, orb_ref, local_ref, near_ref, table):
-    for j in range(BLOCK):
+def deal_near_kernel(pos_ref, orb_ref, near_ref, table):
+    for j in range(ROWS):
         table[:, j, :] = orb_ref[:, j * 128 : (j + 1) * 128]
-    local_ref[...] = table[...]
 
     def here(p, carry):
         for s in range(PAIR_DEV):
@@ -535,17 +558,13 @@
 
 
 def deal_near(pos, orbitals):
-    rows = pl.BlockSpec((128, BLOCK, 128), lambda i: (0, i, 0))
+    vmem = pl.BlockSpec(memory_space=pltpu.VMEM)
     return pl.pallas_call(
         deal_near_kernel,
-        out_shape=[
-            jax.ShapeDtypeStruct((128, ROWS, 128), jnp.float32),
-            jax.ShapeDtypeStruct((B, PAIR_DEV, ROWS, 128), jnp.float32),
-        ],
-        grid=(ROWS // BLOCK,),
-        in_specs=[pl.BlockSpec(memory_space=pltpu.SMEM), pl.BlockSpec((128, BLOCK * 128), lambda i: (0, i))],
-        out_specs=[rows, pl.BlockSpec((B, PAIR_DEV, BLOCK, 128), lambda i: (0, 0, i, 0))],
-        scratch_shapes=[pltpu.VMEM((128, BLOCK, 128), jnp.float32)],
+        out_shape=jax.ShapeDtypeStruct((B, PAIR_DEV, ROWS, 128), jnp.float32),
+        in_specs=[pl.BlockSpec(memory_space=pltpu.SMEM), vmem],
+        out_specs=vmem,
+        scratch_shapes=[pltpu.VMEM((128, ROWS, 128), jnp.float32)],
         compiler_params=pltpu.CompilerParams(vmem_limit_bytes=60 << 20),
         cost_estimate=pl.CostEstimate(flops=2_000_000, bytes_accessed=10_000_000, transcendentals=0),
         name="deal_near",
@@ -575,8 +594,8 @@
 
 
 def fitting(orbitals, anchors, place, pos, slot):
-    local, near = deal_near(pos, orbitals)
-    near = exchanged(near)
+    near = exchanged(deal_near(pos, orbitals))
+    local = orbitals.reshape(128, ROWS, 128)
     sent = fetch(slot, [local], 3, KEEP, sent_row, 0, "send")
     arrived = [turned(x, d) for d, x in enumerate(sent, 1)]
     far = exchanged(*fetch(pos, [local] + arrived, 1, 2 * B, far_row, 0, "deal_far"))

time: 282 us -> 283 us (level)
    cond x8 -> x11, local copies, waits for them, and re-layouts: 4.22 us -> 6.17 us
  transfers between devices with their start and end apart: 9 -> 9, of which waited for: 8 -> 8; matrix products, arithmetic and copies ran while one was open for 0% -> 1% of each run, Pallas kernels for 3% -> 3%
where the time goes in v2:
time: 283 us
  waiting for transfers between devices  131 us (46%)
  blocking collectives  56.9 us (20%)
  Pallas kernels  39.3 us (14%)
  starting transfers between devices  33.7 us (12%)
  between operations  14 us (5%)
  local copies, waits for them, and re-layouts  7.23 us (3%)
    ppermute x6, waiting for transfers between devices, turned(): lax.ppermute(x, 'grp', [(g, (g + shift) % groups) for g in range(groups)])  69.7 us
    all_to_all x3, waiting for transfers between devices, exchanged(): lax.all_to_all(planes.reshape(B, PAIR_DEV, ROWS, 128), 'grid', 0, 0, tile...  61.1 us
    all_to_all x1, blocking collectives, exchanged(): lax.all_to_all(planes.reshape(B, PAIR_DEV, ROWS, 128), 'grid', 0, 0, tile...  56.9 us
    all_to_all x3, starting transfers between devices, exchanged(): lax.all_to_all(planes.reshape(B, PAIR_DEV, ROWS, 128), 'grid', 0, 0, tile...  25.2 us
    pallas_call x1, Pallas kernels, solve(): pl.pallas_call(pair_kernel, out_shape=[jax.ShapeDtypeStruct((B, PAIR_DEV,...  13.2 us
    ppermute x6, starting transfers between devices, turned(): lax.ppermute(x, 'grp', [(g, (g + shift) % groups) for g in range(groups)])  8.56 us
    pallas_call x1, Pallas kernels, add_near(): pl.pallas_call(add_near_kernel, out_shape=jax.ShapeDtypeStruct((128, ROWS...  7.75 us
    cond x11, local copies, waits for them, and re-layouts  6.17 us
  transfers between devices with their start and end apart: 9, of which 8 were waited for; matrix products, arithmetic and copies ran while one was open for 1% of the time, Pallas kernels for 3%

profile of v2, /device:TPU:1, one launch (start us, length us, event | category | flops | bytes accessed | tf_op | source)
XLA Modules:
  0.0 282.7 jit_solution(95301756739294313)
XLA Ops:
  7.2 3.8 %route.1 = (s32[8,128]{1,0:T(8,128)S(1)}, s32[8,256]{1,0:T(8,128)S(1)}, s32[1]{0:T(128)}) custom-call(s32[1]{0:T(128)} %bitcast.20.me_ref, s32[8,256]{1,0:T(8,128)S(1)} %reshape.247.pair_ref), custom_call_target="tpu_custom_call" | custom-call | flops 10000000 | bytes 1000000 | tf_op jit(solution)/shard_map/route/pallas_call | solution.py:223
  11.7 264.1 %conditional.1 = (f32[128,4096]{1,0:T(8,128)}) conditional(s32[]{:T(128)} %bitcast.22, (s32[256,4,2]{0,2,1:T(2,128)}, f32[128,4096]{1,0:T(8,128)}, s32[512,3]{0,1:T(4,128)}) %tuple.26, (s32[]{:T(128)}, s32[512,3]{0,1:T(4,128)}, s32[8,128]{1,0:T(8,128)S(1)}, f32[128,4096]{1,0:T(8,128)}, s32[8,256]{1,0:T(8,128)S(1)}) %tuple.27), branch_computations={%region_0.12_spmd, %region_12.13_spmd} | conditional | flops 106000000 | bytes 185812448 | solution.py:614
  12.0 5.3 %deal_near.1 = f32[64,2,32,128]{3,2,1,0:T(8,128)} custom-call(s32[8,128]{1,0:T(8,128)S(1)} %get-tuple-element.130.pos_ref.idx_ref, f32[128,4096]{1,0:T(8,128)} %get-tuple-element.134.orb_ref), custom_call_target="tpu_custom_call" | custom-call | flops 2000000 | bytes 10000000 | tf_op jit(solution)/shard_map/cond/branch_1_fun/deal_near/pallas_call | solution.py:562
  17.3 13.2 %all-to-all-start = ((f32[64,2,32,128]{3,2,1,0:T(8,128)}), f32[64,2,32,128]{3,2,1,0:T(8,128)S(1)}, u32[]{:S(2)}, u32[]{:S(2)}) async-start(f32[64,2,32,128]{3,2,1,0:T(8,128)} %deal_near.1), calls=%async_computation | async-start | bytes 4194304 | tf_op jit(solution)/shard_map/cond/branch_1_fun/all_to_all | solution.py:593
  30.5 2.0 copy.36
  35.1 2.5 collective-permute-start.1
  38.7 15.1 %collective-permute-done.refs_1_ = f32[48,32,128]{2,1,0:T(8,128)S(1)} collective-permute-done((f32[48,32,128]{2,1,0:T(8,128)S(1)}, f32[48,32,128]{2,1,0:T(8,128)S(1)}, u32[]{:S(2)}, u32[]{:S(2)}) %collective-permute-start) | collective-permute-done | bytes 786464 | tf_op jit(solution)/shard_map/cond/branch_1_fun/ppermute | solution.py:576
  53.7 17.8 %collective-permute-done.1.refs_2_ = f32[48,32,128]{2,1,0:T(8,128)S(1)} collective-permute-done((f32[48,32,128]{2,1,0:T(8,128)S(1)}, f32[48,32,128]{2,1,0:T(8,128)S(1)}, u32[]{:S(2)}, u32[]{:S(2)}) %collective-permute-start.1) | collective-permute-done | bytes 786464 | tf_op jit(solution)/shard_map/cond/branch_1_fun/ppermute | solution.py:576
  71.6 1.6 deal_far.1
  74.5 7.3 %all-to-all-done.near_ref = f32[64,2,32,128]{3,2,1,0:T(8,128)S(1)} async-done(((f32[64,2,32,128]{3,2,1,0:T(8,128)}), f32[64,2,32,128]{3,2,1,0:T(8,128)S(1)}, u32[]{:S(2)}, u32[]{:S(2)}) %all-to-all-start) | async-done | bytes 2097184 | tf_op jit(solution)/shard_map/cond/branch_1_fun/all_to_all | solution.py:593
  81.7 6.0 %all-to-all-start.1 = ((f32[64,2,32,128]{3,2,1,0:T(8,128)}), f32[64,2,32,128]{3,2,1,0:T(8,128)}, u32[]{:S(2)}, u32[]{:S(2)}) async-start(f32[64,2,32,128]{3,2,1,0:T(8,128)} %bitcast.70), calls=%async_computation.1 | async-start | bytes 4194304 | tf_op jit(solution)/shard_map/cond/branch_1_fun/all_to_all | solution.py:593
  88.1 50.8 %all-to-all-done.1.far_ref = f32[64,2,32,128]{3,2,1,0:T(8,128)} async-done(((f32[64,2,32,128]{3,2,1,0:T(8,128)}), f32[64,2,32,128]{3,2,1,0:T(8,128)}, u32[]{:S(2)}, u32[]{:S(2)}) %all-to-all-start.1) | async-done | bytes 2097184 | tf_op jit(solution)/shard_map/cond/branch_1_fun/all_to_all | solution.py:593
  138.9 13.2 %solve.1 = (f32[64,2,32,128]{3,2,1,0:T(8,128)S(1)}, f32[64,2,32,128]{3,2,1,0:T(8,128)S(1)}) custom-call(s32[1]{0:T(128)} %bitcast.17.place_ref, s32[8,128]{1,0:T(8,128)S(1)} %get-tuple-element.130.pos_ref.idx_ref, s32[1536]{0:T(1024)S(1)} %reshape.242.anchor_ref, f32[64,2,32,128]{3,2,1,0:T(8,128)S(1)} %all-to-all-done.near_ref, ...), custom_call_target="tpu_custom_call" | custom-call | flops 100000000 | bytes 30000000 | tf_op jit(solution)/shard_map/cond/branch_1_fun/solve/pallas_call | solution.py:456
  152.1 56.9 %all_to_all.24.terms_ref = f32[64,2,32,128]{3,2,1,0:T(8,128)S(1)} all-to-all(f32[64,2,32,128]{3,2,1,0:T(8,128)S(1)} %get-tuple-element.138), channel_id=1, replica_groups=mesh['grp'=4,'grid'=64] {'grid'}, dimensions={0} | all-to-all | bytes 4194304 | tf_op jit(solution)/shard_map/cond/branch_1_fun/all_to_all | solution.py:593
  209.0 6.0 %all-to-all-start.3 = ((f32[64,2,32,128]{3,2,1,0:T(8,128)}), f32[64,2,32,128]{3,2,1,0:T(8,128)}, u32[]{:S(2)}, u32[]{:S(2)}) async-start(f32[64,2,32,128]{3,2,1,0:T(8,128)} %copy-done.3), calls=%async_computation.3 | async-start | bytes 4194304 | tf_op jit(solution)/shard_map/cond/branch_1_fun/all_to_all | solution.py:593
  215.0 1.5 back.1
  216.6 2.6 collective-permute-start.3
  220.3 16.1 %collective-permute-done.3.refs_0_ = f32[48,32,128]{2,1,0:T(8,128)S(1)} collective-permute-done((f32[48,32,128]{2,1,0:T(8,128)S(1)}, f32[48,32,128]{2,1,0:T(8,128)S(1)}, u32[]{:S(2)}, u32[]{:S(2)}) %collective-permute-start.3) | collective-permute-done | bytes 786464 | tf_op jit(solution)/shard_map/cond/branch_1_fun/ppermute | solution.py:576
  236.3 2.7 collective-permute-done.4.refs_1_
  239.0 18.0 %collective-permute-done.5.refs_2_ = f32[48,32,128]{2,1,0:T(8,128)S(1)} collective-permute-done((f32[48,32,128]{2,1,0:T(8,128)S(1)}, f32[48,32,128]{2,1,0:T(8,128)S(1)}, u32[]{:S(2)}, u32[]{:S(2)}) %collective-permute-start.5) | collective-permute-done | bytes 786464 | tf_op jit(solution)/shard_map/cond/branch_1_fun/ppermute | solution.py:576
  257.1 4.7 %add_far.1.sum_ref = f32[128,32,128]{2,1,0:T(8,128)S(1)} custom-call(s32[8,128]{1,0:T(8,128)S(1)} %get-tuple-element.130.pos_ref.idx_ref, s32[8,256]{1,0:T(8,128)S(1)} %get-tuple-element.131.idx_ref.slot_ref, f32[64,2,32,128]{3,2,1,0:T(8,128)S(1)} %all_to_all.24.terms_ref, f32[48,32,128]{2,1,0:T(8,128)S(1)} %collective-permute-done.3.refs_0_, ...), custom_call_target="tpu_custom_call" | custom-call | flops 2000000 | bytes 10000000 | tf_op jit(solution)/shard_map/cond/branch_1_fun/add_far/pallas_call | solution.py:500
  263.1 3.1 %all-to-all-done.3.terms_ref = f32[64,2,32,128]{3,2,1,0:T(8,128)} async-done(((f32[64,2,32,128]{3,2,1,0:T(8,128)}), f32[64,2,32,128]{3,2,1,0:T(8,128)}, u32[]{:S(2)}, u32[]{:S(2)}) %all-to-all-start.3) | async-done | bytes 2097184 | tf_op jit(solution)/shard_map/cond/branch_1_fun/all_to_all | solution.py:593
  266.2 1.6 copy-done.2
  267.8 7.7 %add_near.1 = f32[128,4096]{1,0:T(8,128)} custom-call(s32[8,128]{1,0:T(8,128)S(1)} %get-tuple-element.130.pos_ref.idx_ref, f32[128,32,128]{2,1,0:T(8,128)S(1)} %copy-done.2, f32[64,2,32,128]{3,2,1,0:T(8,128)} %all-to-all-done.3.terms_ref), custom_call_target="tpu_custom_call" | custom-call | flops 2000000 | bytes 10000000 | tf_op jit(solution)/shard_map/cond/branch_1_fun/add_near/pallas_call | solution.py:536
  (18 shorter events, 8.6 us)
Async XLA Ops:
  17.3 64.4 %all-to-all-start = ((f32[64,2,32,128]{3,2,1,0:T(8,128)}), f32[64,2,32,128]{3,2,1,0:T(8,128)S(1)}, u32[]{:S(2)}, u32[]{:S(2)}) async-start(f32[64,2,32,128]{3,2,1,0:T(8,128)} %deal_near.1), calls=%async_computation | async-start | bytes 4194304 | tf_op jit(solution)/shard_map/cond/branch_1_fun/all_to_all | solution.py:593
  33.8 19.9 %collective-permute-start = (f32[48,32,128]{2,1,0:T(8,128)S(1)}, f32[48,32,128]{2,1,0:T(8,128)S(1)}, u32[]{:S(2)}, u32[]{:S(2)}) collective-permute-start(f32[48,32,128]{2,1,0:T(8,128)S(1)} %get-tuple-element.135), channel_id=1, source_target_pairs={{0,64},{64,128},{128,192},{192,0},{1,65},{65,129},{129,193},{193,1... | collective-permute-start | bytes 2359304 | tf_op jit(solution)/shard_map/cond/branch_1_fun/ppermute | solution.py:576
  35.1 36.5 %collective-permute-start.1 = (f32[48,32,128]{2,1,0:T(8,128)S(1)}, f32[48,32,128]{2,1,0:T(8,128)S(1)}, u32[]{:S(2)}, u32[]{:S(2)}) collective-permute-start(f32[48,32,128]{2,1,0:T(8,128)S(1)} %get-tuple-element.136), channel_id=1, source_target_pairs={{0,128},{64,192},{128,0},{192,64},{1,129},{65,193},{129,1},{193,65... | collective-permute-start | bytes 2359304 | tf_op jit(solution)/shard_map/cond/branch_1_fun/ppermute | solution.py:576
  37.5 34.1 %collective-permute-start.2 = (f32[48,32,128]{2,1,0:T(8,128)S(1)}, f32[48,32,128]{2,1,0:T(8,128)S(1)}, u32[]{:S(2)}, u32[]{:S(2)}) collective-permute-start(f32[48,32,128]{2,1,0:T(8,128)S(1)} %get-tuple-element.137), channel_id=1, source_target_pairs={{0,192},{64,0},{128,64},{192,128},{1,193},{65,1},{129,65},{193,129... | collective-permute-start | bytes 2359304 | tf_op jit(solution)/shard_map/cond/branch_1_fun/ppermute | solution.py:576
  73.1 1.3 copy-start
  74.5 13.3 %copy-start.8 = (s32[512,3]{0,1:T(4,128)S(1)}, s32[512,3]{0,1:T(4,128)}, u32[]{:S(2)}) copy-start(s32[512,3]{0,1:T(4,128)} %get-tuple-element.196) | copy-start | bytes 18436 | tf_op jit(solution)/shard_map/cond
  81.7 57.2 %all-to-all-start.1 = ((f32[64,2,32,128]{3,2,1,0:T(8,128)}), f32[64,2,32,128]{3,2,1,0:T(8,128)}, u32[]{:S(2)}, u32[]{:S(2)}) async-start(f32[64,2,32,128]{3,2,1,0:T(8,128)} %bitcast.70), calls=%async_computation.1 | async-start | bytes 4194304 | tf_op jit(solution)/shard_map/cond/branch_1_fun/all_to_all | solution.py:593
  152.1 56.9 %copy-start.3 = (f32[64,2,32,128]{3,2,1,0:T(8,128)}, f32[64,2,32,128]{3,2,1,0:T(8,128)S(1)}, u32[]{:S(2)}) copy-start(f32[64,2,32,128]{3,2,1,0:T(8,128)S(1)} %get-tuple-element.142) | copy-start | bytes 6291460 | tf_op jit(solution)/shard_map/cond
  209.0 57.2 %all-to-all-start.3 = ((f32[64,2,32,128]{3,2,1,0:T(8,128)}), f32[64,2,32,128]{3,2,1,0:T(8,128)}, u32[]{:S(2)}, u32[]{:S(2)}) async-start(f32[64,2,32,128]{3,2,1,0:T(8,128)} %copy-done.3), calls=%async_computation.3 | async-start | bytes 4194304 | tf_op jit(solution)/shard_map/cond/branch_1_fun/all_to_all | solution.py:593
  216.6 19.7 %collective-permute-start.3 = (f32[48,32,128]{2,1,0:T(8,128)S(1)}, f32[48,32,128]{2,1,0:T(8,128)S(1)}, u32[]{:S(2)}, u32[]{:S(2)}) collective-permute-start(f32[48,32,128]{2,1,0:T(8,128)S(1)} %get-tuple-element.139), channel_id=1, source_target_pairs={{0,192},{64,0},{128,64},{192,128},{1,193},{65,1},{129,65},{193,129... | collective-permute-start | bytes 2359304 | tf_op jit(solution)/shard_map/cond/branch_1_fun/ppermute | solution.py:576
  219.1 19.9 %collective-permute-start.4 = (f32[48,32,128]{2,1,0:T(8,128)S(1)}, f32[48,32,128]{2,1,0:T(8,128)S(1)}, u32[]{:S(2)}, u32[]{:S(2)}) collective-permute-start(f32[48,32,128]{2,1,0:T(8,128)S(1)} %get-tuple-element.140), channel_id=1, source_target_pairs={{0,128},{64,192},{128,0},{192,64},{1,129},{65,193},{129,1},{193,65... | collective-permute-start | bytes 2359304 | tf_op jit(solution)/shard_map/cond/branch_1_fun/ppermute | solution.py:576
  219.7 37.3 %collective-permute-start.5 = (f32[48,32,128]{2,1,0:T(8,128)S(1)}, f32[48,32,128]{2,1,0:T(8,128)S(1)}, u32[]{:S(2)}, u32[]{:S(2)}) collective-permute-start(f32[48,32,128]{2,1,0:T(8,128)S(1)} %get-tuple-element.141), channel_id=1, source_target_pairs={{0,64},{64,128},{128,192},{192,0},{1,65},{65,129},{129,193},{193,1... | collective-permute-start | bytes 2359304 | tf_op jit(solution)/shard_map/cond/branch_1_fun/ppermute | solution.py:576
  261.8 1.3 copy-start.1
  266.2 1.6 copy-start.2

commit v3 on v2

--- a/solution.py
+++ b/solution.py
@@ -13,6 +13,7 @@
 ROWS = B * B // 128
 KEEP = 48
 UNROLL = 16
+BLOCK = 16
 
 
 def shift_field(field, offset, extent):
@@ -508,46 +509,55 @@
     )(pos, slot, terms, *from_groups)
 
 
-def add_near_kernel(pos_ref, sum_ref, terms_ref, out_ref, terms, first, second, sem):
-    copies = [
-        pltpu.make_async_copy(terms_ref, terms, sem.at[0]),
-        pltpu.make_async_copy(sum_ref, first, sem.at[1]),
-    ]
-    for copy in copies:
-        copy.start()
-    second[...] = jnp.zeros(second.shape, jnp.float32)
-    for copy in copies:
-        copy.wait()
+def add_near_kernel(pos_ref, sum_ref, terms_ref, out_ref, acc):
+    acc[...] = sum_ref[...]
 
     def here(p, carry):
-        for s, total in enumerate((first, second)):
+        for s in range(PAIR_DEV):
             j = pos_ref[0, s * B + p]
-            total[j] = total[j] + terms[p, s]
+            acc[j] = acc[j] + terms_ref[p, s]
         return carry
 
     lax.fori_loop(0, B, here, 0, unroll=4)
-    for j in range(ROWS):
-        out_ref[:, j * 128 : (j + 1) * 128] = first[:, j, :] + second[:, j, :]
+
+    def lay_out(k, carry):
+        rows = pl.ds(pl.multiple_of(k * 8, 8), 8)
+        for first in range(0, BLOCK, 8):
+            lines = jnp.swapaxes(acc[rows, first : first + 8], 0, 1)
+            for j in range(8):
+                out_ref[rows, (first + j) * 128 : (first + j + 1) * 128] = lines[j]
+        return carry
+
+    lax.fori_loop(0, acc.shape[0] // 8, lay_out, 0, unroll=2)
 
 
 def add_near(pos, summed, terms):
-    anywhere = pl.BlockSpec(memory_space=pl.ANY)
-    total = pltpu.VMEM((128, ROWS, 128), jnp.float32)
     return pl.pallas_call(
         add_near_kernel,
         out_shape=jax.ShapeDtypeStruct((128, ROWS * 128), jnp.float32),
-        in_specs=[pl.BlockSpec(memory_space=pltpu.SMEM), anywhere, anywhere],
-        out_specs=pl.BlockSpec(memory_space=pltpu.VMEM),
-        scratch_shapes=[pltpu.VMEM((B, PAIR_DEV, ROWS, 128), jnp.float32), total, total, pltpu.SemaphoreType.DMA((2,))],
-        compiler_params=pltpu.CompilerParams(vmem_limit_bytes=24 << 20),
+        grid=(ROWS // BLOCK,),
+        in_specs=[
+            pl.BlockSpec(memory_space=pltpu.SMEM),
+            pl.BlockSpec((128, BLOCK, 128), lambda i: (0, i, 0)),
+            pl.BlockSpec((B, PAIR_DEV, BLOCK, 128), lambda i: (0, 0, i, 0)),
+        ],
+        out_specs=pl.BlockSpec((128, BLOCK * 128), lambda i: (0, i)),
+        scratch_shapes=[pltpu.VMEM((128, BLOCK, 128), jnp.float32)],
+        compiler_params=pltpu.CompilerParams(vmem_limit_bytes=60 << 20),
         cost_estimate=pl.CostEstimate(flops=2_000_000, bytes_accessed=10_000_000, transcendentals=0),
         name="add_near",
     )(pos, summed, terms)
 
 
 def deal_near_kernel(pos_ref, orb_ref, near_ref, table):
-    for j in range(ROWS):
-        table[:, j, :] = orb_ref[:, j * 128 : (j + 1) * 128]
+    def lay_out(k, carry):
+        rows = pl.ds(pl.multiple_of(k * 8, 8), 8)
+        for first in range(0, BLOCK, 8):
+            lines = [orb_ref[rows, (first + j) * 128 : (first + j + 1) * 128] for j in range(8)]
+            table[rows, first : first + 8] = jnp.swapaxes(jnp.stack(lines), 0, 1)
+        return carry
+
+    lax.fori_loop(0, table.shape[0] // 8, lay_out, 0, unroll=2)
 
     def here(p, carry):
         for s in range(PAIR_DEV):
@@ -558,13 +568,13 @@
 
 
 def deal_near(pos, orbitals):
-    vmem = pl.BlockSpec(memory_space=pltpu.VMEM)
     return pl.pallas_call(
         deal_near_kernel,
         out_shape=jax.ShapeDtypeStruct((B, PAIR_DEV, ROWS, 128), jnp.float32),
-        in_specs=[pl.BlockSpec(memory_space=pltpu.SMEM), vmem],
-        out_specs=vmem,
-        scratch_shapes=[pltpu.VMEM((128, ROWS, 128), jnp.float32)],
+        grid=(ROWS // BLOCK,),
+        in_specs=[pl.BlockSpec(memory_space=pltpu.SMEM), pl.BlockSpec((128, BLOCK * 128), lambda i: (0, i))],
+        out_specs=pl.BlockSpec((B, PAIR_DEV, BLOCK, 128), lambda i: (0, 0, i, 0)),
+        scratch_shapes=[pltpu.VMEM((128, BLOCK, 128), jnp.float32)],
         compiler_params=pltpu.CompilerParams(vmem_limit_bytes=60 << 20),
         cost_estimate=pl.CostEstimate(flops=2_000_000, bytes_accessed=10_000_000, transcendentals=0),
         name="deal_near",

time: 283 us -> 275 us (0.972)
  Pallas kernels: 39.3 us -> 33.5 us
    pallas_call x1, Pallas kernels: 7.75 us -> 4.1 us  [add_near(): pl.pallas_call(add_near_kernel, out_shape=jax.ShapeDtypeStruct((128, ROWS...]
    cond x11 -> x9, local copies, waits for them, and re-layouts: 6.17 us -> 4.58 us
where the time goes in v3:
time: 275 us
  waiting for transfers between devices  131 us (48%)
  blocking collectives  56.9 us (21%)
  starting transfers between devices  33.7 us (12%)
  Pallas kernels  33.5 us (12%)
  between operations  14 us (5%)
  local copies, waits for them, and re-layouts  5.64 us (2%)
    ppermute x6, waiting for transfers between devices, turned(): lax.ppermute(x, 'grp', [(g, (g + shift) % groups) for g in range(groups)])  69.7 us
    all_to_all x3, waiting for transfers between devices, exchanged(): lax.all_to_all(planes.reshape(B, PAIR_DEV, ROWS, 128), 'grid', 0, 0, tile...  61.1 us
    all_to_all x1, blocking collectives, exchanged(): lax.all_to_all(planes.reshape(B, PAIR_DEV, ROWS, 128), 'grid', 0, 0, tile...  56.9 us
    all_to_all x3, starting transfers between devices, exchanged(): lax.all_to_all(planes.reshape(B, PAIR_DEV, ROWS, 128), 'grid', 0, 0, tile...  25.2 us
    pallas_call x1, Pallas kernels, solve(): pl.pallas_call(pair_kernel, out_shape=[jax.ShapeDtypeStruct((B, PAIR_DEV,...  13.2 us
    ppermute x6, starting transfers between devices, turned(): lax.ppermute(x, 'grp', [(g, (g + shift) % groups) for g in range(groups)])  8.55 us
  transfers between devices with their start and end apart: 9, of which 8 were waited for; matrix products, arithmetic and copies ran while one was open for 1% of the time, Pallas kernels for 3%

profile of v3, /device:TPU:1, one launch (start us, length us, event | category | flops | bytes accessed | tf_op | source)
XLA Modules:
  0.0 274.9 jit_solution(2728411676473120868)
XLA Ops:
  7.2 3.8 %route.1 = (s32[8,128]{1,0:T(8,128)S(1)}, s32[8,256]{1,0:T(8,128)S(1)}, s32[1]{0:T(128)}) custom-call(s32[1]{0:T(128)} %bitcast.20.me_ref, s32[8,256]{1,0:T(8,128)S(1)} %reshape.247.pair_ref), custom_call_target="tpu_custom_call" | custom-call | flops 10000000 | bytes 1000000 | tf_op jit(solution)/shard_map/route/pallas_call | solution.py:224
  11.7 256.3 %conditional.1 = (f32[128,4096]{1,0:T(8,128)}) conditional(s32[]{:T(128)} %bitcast.22, (s32[256,4,2]{0,2,1:T(2,128)}, f32[128,4096]{1,0:T(8,128)}, s32[512,3]{0,1:T(4,128)}) %tuple.26, (s32[]{:T(128)}, s32[512,3]{0,1:T(4,128)}, s32[8,128]{1,0:T(8,128)S(1)}, f32[128,4096]{1,0:T(8,128)}, s32[8,256]{1,0:T(8,128)S(1)}) %tuple.27), branch_computations={%region_0.12_spmd, %region_12.13_spmd} | conditional | flops 106000000 | bytes 185812448 | solution.py:624
  11.9 3.1 %deal_near.1 = f32[64,2,32,128]{3,2,1,0:T(8,128)} custom-call(s32[8,128]{1,0:T(8,128)S(1)} %get-tuple-element.130.pos_ref.idx_ref, f32[128,4096]{1,0:T(8,128)} %get-tuple-element.134.orb_ref), custom_call_target="tpu_custom_call" | custom-call | flops 2000000 | bytes 10000000 | tf_op jit(solution)/shard_map/cond/branch_1_fun/deal_near/pallas_call | solution.py:571
  15.0 13.2 %all-to-all-start = ((f32[64,2,32,128]{3,2,1,0:T(8,128)}), f32[64,2,32,128]{3,2,1,0:T(8,128)S(1)}, u32[]{:S(2)}, u32[]{:S(2)}) async-start(f32[64,2,32,128]{3,2,1,0:T(8,128)} %deal_near.1), calls=%async_computation | async-start | bytes 4194304 | tf_op jit(solution)/shard_map/cond/branch_1_fun/all_to_all | solution.py:603
  28.2 2.0 copy.36
  30.2 1.3 send.1
  32.8 2.5 collective-permute-start.1
  36.4 15.1 %collective-permute-done.refs_1_ = f32[48,32,128]{2,1,0:T(8,128)S(1)} collective-permute-done((f32[48,32,128]{2,1,0:T(8,128)S(1)}, f32[48,32,128]{2,1,0:T(8,128)S(1)}, u32[]{:S(2)}, u32[]{:S(2)}) %collective-permute-start) | collective-permute-done | bytes 786464 | tf_op jit(solution)/shard_map/cond/branch_1_fun/ppermute | solution.py:586
  51.5 17.8 %collective-permute-done.1.refs_2_ = f32[48,32,128]{2,1,0:T(8,128)S(1)} collective-permute-done((f32[48,32,128]{2,1,0:T(8,128)S(1)}, f32[48,32,128]{2,1,0:T(8,128)S(1)}, u32[]{:S(2)}, u32[]{:S(2)}) %collective-permute-start.1) | collective-permute-done | bytes 786464 | tf_op jit(solution)/shard_map/cond/branch_1_fun/ppermute | solution.py:586
  69.3 1.6 deal_far.1
  72.2 7.2 %all-to-all-done.near_ref = f32[64,2,32,128]{3,2,1,0:T(8,128)S(1)} async-done(((f32[64,2,32,128]{3,2,1,0:T(8,128)}), f32[64,2,32,128]{3,2,1,0:T(8,128)S(1)}, u32[]{:S(2)}, u32[]{:S(2)}) %all-to-all-start) | async-done | bytes 2097184 | tf_op jit(solution)/shard_map/cond/branch_1_fun/all_to_all | solution.py:603
  79.4 6.0 %all-to-all-start.1 = ((f32[64,2,32,128]{3,2,1,0:T(8,128)}), f32[64,2,32,128]{3,2,1,0:T(8,128)}, u32[]{:S(2)}, u32[]{:S(2)}) async-start(f32[64,2,32,128]{3,2,1,0:T(8,128)} %bitcast.70), calls=%async_computation.1 | async-start | bytes 4194304 | tf_op jit(solution)/shard_map/cond/branch_1_fun/all_to_all | solution.py:603
  85.8 50.8 %all-to-all-done.1.far_ref = f32[64,2,32,128]{3,2,1,0:T(8,128)} async-done(((f32[64,2,32,128]{3,2,1,0:T(8,128)}), f32[64,2,32,128]{3,2,1,0:T(8,128)}, u32[]{:S(2)}, u32[]{:S(2)}) %all-to-all-start.1) | async-done | bytes 2097184 | tf_op jit(solution)/shard_map/cond/branch_1_fun/all_to_all | solution.py:603
  136.6 13.2 %solve.1 = (f32[64,2,32,128]{3,2,1,0:T(8,128)S(1)}, f32[64,2,32,128]{3,2,1,0:T(8,128)S(1)}) custom-call(s32[1]{0:T(128)} %bitcast.17.place_ref, s32[8,128]{1,0:T(8,128)S(1)} %get-tuple-element.130.pos_ref.idx_ref, s32[1536]{0:T(1024)S(1)} %reshape.242.anchor_ref, f32[64,2,32,128]{3,2,1,0:T(8,128)S(1)} %all-to-all-done.near_ref, ...), custom_call_target="tpu_custom_call" | custom-call | flops 100000000 | bytes 30000000 | tf_op jit(solution)/shard_map/cond/branch_1_fun/solve/pallas_call | solution.py:457
  149.9 56.9 %all_to_all.24.terms_ref = f32[64,2,32,128]{3,2,1,0:T(8,128)S(1)} all-to-all(f32[64,2,32,128]{3,2,1,0:T(8,128)S(1)} %get-tuple-element.138), channel_id=1, replica_groups=mesh['grp'=4,'grid'=64] {'grid'}, dimensions={0} | all-to-all | bytes 4194304 | tf_op jit(solution)/shard_map/cond/branch_1_fun/all_to_all | solution.py:603
  206.8 6.0 %all-to-all-start.3 = ((f32[64,2,32,128]{3,2,1,0:T(8,128)}), f32[64,2,32,128]{3,2,1,0:T(8,128)}, u32[]{:S(2)}, u32[]{:S(2)}) async-start(f32[64,2,32,128]{3,2,1,0:T(8,128)} %copy-done.2), calls=%async_computation.3 | async-start | bytes 4194304 | tf_op jit(solution)/shard_map/cond/branch_1_fun/all_to_all | solution.py:603
  212.8 1.5 back.1
  214.3 2.6 collective-permute-start.3
  218.0 16.1 %collective-permute-done.3.refs_0_ = f32[48,32,128]{2,1,0:T(8,128)S(1)} collective-permute-done((f32[48,32,128]{2,1,0:T(8,128)S(1)}, f32[48,32,128]{2,1,0:T(8,128)S(1)}, u32[]{:S(2)}, u32[]{:S(2)}) %collective-permute-start.3) | collective-permute-done | bytes 786464 | tf_op jit(solution)/shard_map/cond/branch_1_fun/ppermute | solution.py:586
  234.0 2.7 collective-permute-done.4.refs_1_
  236.8 18.0 %collective-permute-done.5.refs_2_ = f32[48,32,128]{2,1,0:T(8,128)S(1)} collective-permute-done((f32[48,32,128]{2,1,0:T(8,128)S(1)}, f32[48,32,128]{2,1,0:T(8,128)S(1)}, u32[]{:S(2)}, u32[]{:S(2)}) %collective-permute-start.5) | collective-permute-done | bytes 786464 | tf_op jit(solution)/shard_map/cond/branch_1_fun/ppermute | solution.py:586
  254.8 4.8 %add_far.1.sum_ref = f32[128,32,128]{2,1,0:T(8,128)S(1)} custom-call(s32[8,128]{1,0:T(8,128)S(1)} %get-tuple-element.130.pos_ref.idx_ref, s32[8,256]{1,0:T(8,128)S(1)} %get-tuple-element.131.idx_ref.slot_ref, f32[64,2,32,128]{3,2,1,0:T(8,128)S(1)} %all_to_all.24.terms_ref, f32[48,32,128]{2,1,0:T(8,128)S(1)} %collective-permute-done.3.refs_0_, ...), custom_call_target="tpu_custom_call" | custom-call | flops 2000000 | bytes 10000000 | tf_op jit(solution)/shard_map/cond/branch_1_fun/add_far/pallas_call | solution.py:501
  260.9 3.1 %all-to-all-done.3.terms_ref = f32[64,2,32,128]{3,2,1,0:T(8,128)} async-done(((f32[64,2,32,128]{3,2,1,0:T(8,128)}), f32[64,2,32,128]{3,2,1,0:T(8,128)}, u32[]{:S(2)}, u32[]{:S(2)}) %all-to-all-start.3) | async-done | bytes 2097184 | tf_op jit(solution)/shard_map/cond/branch_1_fun/all_to_all | solution.py:603
  263.9 4.1 %add_near.1 = f32[128,4096]{1,0:T(8,128)} custom-call(s32[8,128]{1,0:T(8,128)S(1)} %get-tuple-element.130.pos_ref.idx_ref, f32[128,32,128]{2,1,0:T(8,128)} %copy-done.1, f32[64,2,32,128]{3,2,1,0:T(8,128)} %all-to-all-done.3.terms_ref), custom_call_target="tpu_custom_call" | custom-call | flops 2000000 | bytes 10000000 | tf_op jit(solution)/shard_map/cond/branch_1_fun/add_near/pallas_call | solution.py:535
  (16 shorter events, 7.2 us)
Async XLA Ops:
  15.0 64.4 %all-to-all-start = ((f32[64,2,32,128]{3,2,1,0:T(8,128)}), f32[64,2,32,128]{3,2,1,0:T(8,128)S(1)}, u32[]{:S(2)}, u32[]{:S(2)}) async-start(f32[64,2,32,128]{3,2,1,0:T(8,128)} %deal_near.1), calls=%async_computation | async-start | bytes 4194304 | tf_op jit(solution)/shard_map/cond/branch_1_fun/all_to_all | solution.py:603
  31.5 19.9 %collective-permute-start = (f32[48,32,128]{2,1,0:T(8,128)S(1)}, f32[48,32,128]{2,1,0:T(8,128)S(1)}, u32[]{:S(2)}, u32[]{:S(2)}) collective-permute-start(f32[48,32,128]{2,1,0:T(8,128)S(1)} %get-tuple-element.135), channel_id=1, source_target_pairs={{0,64},{64,128},{128,192},{192,0},{1,65},{65,129},{129,193},{193,1... | collective-permute-start | bytes 2359304 | tf_op jit(solution)/shard_map/cond/branch_1_fun/ppermute | solution.py:586
  32.8 36.5 %collective-permute-start.1 = (f32[48,32,128]{2,1,0:T(8,128)S(1)}, f32[48,32,128]{2,1,0:T(8,128)S(1)}, u32[]{:S(2)}, u32[]{:S(2)}) collective-permute-start(f32[48,32,128]{2,1,0:T(8,128)S(1)} %get-tuple-element.136), channel_id=1, source_target_pairs={{0,128},{64,192},{128,0},{192,64},{1,129},{65,193},{129,1},{193,65... | collective-permute-start | bytes 2359304 | tf_op jit(solution)/shard_map/cond/branch_1_fun/ppermute | solution.py:586
  35.3 34.1 %collective-permute-start.2 = (f32[48,32,128]{2,1,0:T(8,128)S(1)}, f32[48,32,128]{2,1,0:T(8,128)S(1)}, u32[]{:S(2)}, u32[]{:S(2)}) collective-permute-start(f32[48,32,128]{2,1,0:T(8,128)S(1)} %get-tuple-element.137), channel_id=1, source_target_pairs={{0,192},{64,0},{128,64},{192,128},{1,193},{65,1},{129,65},{193,129... | collective-permute-start | bytes 2359304 | tf_op jit(solution)/shard_map/cond/branch_1_fun/ppermute | solution.py:586
  70.9 1.3 copy-start
  72.2 13.3 %copy-start.7 = (s32[512,3]{0,1:T(4,128)S(1)}, s32[512,3]{0,1:T(4,128)}, u32[]{:S(2)}) copy-start(s32[512,3]{0,1:T(4,128)} %get-tuple-element.196) | copy-start | bytes 18436 | tf_op jit(solution)/shard_map/cond
  79.4 57.2 %all-to-all-start.1 = ((f32[64,2,32,128]{3,2,1,0:T(8,128)}), f32[64,2,32,128]{3,2,1,0:T(8,128)}, u32[]{:S(2)}, u32[]{:S(2)}) async-start(f32[64,2,32,128]{3,2,1,0:T(8,128)} %bitcast.70), calls=%async_computation.1 | async-start | bytes 4194304 | tf_op jit(solution)/shard_map/cond/branch_1_fun/all_to_all | solution.py:603
  149.9 56.9 %copy-start.2 = (f32[64,2,32,128]{3,2,1,0:T(8,128)}, f32[64,2,32,128]{3,2,1,0:T(8,128)S(1)}, u32[]{:S(2)}) copy-start(f32[64,2,32,128]{3,2,1,0:T(8,128)S(1)} %get-tuple-element.142) | copy-start | bytes 6291460 | tf_op jit(solution)/shard_map/cond
  206.8 57.2 %all-to-all-start.3 = ((f32[64,2,32,128]{3,2,1,0:T(8,128)}), f32[64,2,32,128]{3,2,1,0:T(8,128)}, u32[]{:S(2)}, u32[]{:S(2)}) async-start(f32[64,2,32,128]{3,2,1,0:T(8,128)} %copy-done.2), calls=%async_computation.3 | async-start | bytes 4194304 | tf_op jit(solution)/shard_map/cond/branch_1_fun/all_to_all | solution.py:603
  214.3 19.7 %collective-permute-start.3 = (f32[48,32,128]{2,1,0:T(8,128)S(1)}, f32[48,32,128]{2,1,0:T(8,128)S(1)}, u32[]{:S(2)}, u32[]{:S(2)}) collective-permute-start(f32[48,32,128]{2,1,0:T(8,128)S(1)} %get-tuple-element.139), channel_id=1, source_target_pairs={{0,192},{64,0},{128,64},{192,128},{1,193},{65,1},{129,65},{193,129... | collective-permute-start | bytes 2359304 | tf_op jit(solution)/shard_map/cond/branch_1_fun/ppermute | solution.py:586
  216.9 19.9 %collective-permute-start.4 = (f32[48,32,128]{2,1,0:T(8,128)S(1)}, f32[48,32,128]{2,1,0:T(8,128)S(1)}, u32[]{:S(2)}, u32[]{:S(2)}) collective-permute-start(f32[48,32,128]{2,1,0:T(8,128)S(1)} %get-tuple-element.140), channel_id=1, source_target_pairs={{0,128},{64,192},{128,0},{192,64},{1,129},{65,193},{129,1},{193,65... | collective-permute-start | bytes 2359304 | tf_op jit(solution)/shard_map/cond/branch_1_fun/ppermute | solution.py:586
  217.4 37.4 %collective-permute-start.5 = (f32[48,32,128]{2,1,0:T(8,128)S(1)}, f32[48,32,128]{2,1,0:T(8,128)S(1)}, u32[]{:S(2)}, u32[]{:S(2)}) collective-permute-start(f32[48,32,128]{2,1,0:T(8,128)S(1)} %get-tuple-element.141), channel_id=1, source_target_pairs={{0,64},{64,128},{128,192},{192,0},{1,65},{65,129},{129,193},{193,1... | collective-permute-start | bytes 2359304 | tf_op jit(solution)/shard_map/cond/branch_1_fun/ppermute | solution.py:586
  259.6 1.3 copy-start.1
